TPU v7x, 128 devices: a whole 4x4x4 slice. The times are simulated.
128 devices in a mesh: seq: 64 (over z, x, y), head: 2 (over core).
Axes of the slice: x: 4, y: 4, z: 4, core: 2. Of those that a mesh axis runs over, the one named last changes fastest.
Arguments:
- hidden_in: bfloat16 [16384, 1024], P('seq'), may hold values from -16 to 16
- norm1_gain: float32 [1024], replicated, may hold values from 0.5 to 1.5
- in_weight: bfloat16 [1024, 3, 1024], P(None, None, 'head'), may hold values from -0.1875 to 0.1875
- conv_weight: float32 [1024, 3], P('head'), may hold values from -3.5 to 3.5
- out_weight: bfloat16 [1024, 1024], P('head'), may hold values from -0.1875 to 0.1875
- norm2_gain: float32 [1024], replicated, may hold values from 0.5 to 1.5
- gate_weight: bfloat16 [1024, 4608], P(None, 'head'), may hold values from -0.1875 to 0.1875
- up_weight: bfloat16 [1024, 4608], P(None, 'head'), may hold values from -0.1875 to 0.1875
- down_weight: bfloat16 [4608, 1024], P('head'), may hold values from -0.09375 to 0.09375
- cotangent: bfloat16 [16384, 1024], P('seq'), may hold values from -6 to 6
Outputs:
- block_out: bfloat16 [16384, 1024], P('seq')
- input_grad: bfloat16 [16384, 1024], P('seq')
- norm1_gain_grad: float32 [1024], P('seq')
- in_weight_grad: float32 [1024, 3, 1024], P('seq', None, 'head')
- conv_weight_grad: float32 [1024, 3], P(('head', 'seq'))
- out_weight_grad: float32 [1024, 1024], P(('head', 'seq'))
- norm2_gain_grad: float32 [1024], P('seq')
- gate_weight_grad: float32 [1024, 4608], P('seq', 'head')
- up_weight_grad: float32 [1024, 4608], P('seq', 'head')
- down_weight_grad: float32 [4608, 1024], P(('head', 'seq'))
All inputs are finite; a program needn't handle non-finite values.
Results may differ from a plain program's by a relative error of at most 0.019.
Values may be sent and summed in bfloat16 or wider, within the bound.
A program may use at most 192 MiB of HBM per device.

v0:
```python
import jax
import jax.numpy as jnp
from jax import lax
from jax.sharding import PartitionSpec as P

SEQ_BASE = 4096


EPS = 1e-05


def passed_along(value, axis, steps):
    count = lax.axis_size(axis)
    initial, last = (max(0, -steps), min(count, count - steps))
    return lax.ppermute(value, axis, [(source, source + steps) for source in range(initial, last)])


def rms_scale(values):
    return lax.rsqrt(jnp.mean(values * values, axis=-1, keepdims=True) + EPS)


def norm_back(unit_grad, unit, scale):
    return scale * (unit_grad - unit * jnp.mean(unit_grad * unit, axis=-1, keepdims=True))


def shards(
    hidden_in,
    norm1_gain,
    in_weight,
    conv_weight,
    out_weight,
    norm2_gain,
    gate_weight,
    up_weight,
    down_weight,
    cotangent,
):
    tokens_here = hidden_in.shape[0]
    features = hidden_in.shape[1]
    channels = in_weight.shape[2]
    f32 = jnp.float32
    bf16 = jnp.bfloat16
    seq_length = min(SEQ_BASE, tokens_here * lax.axis_size("seq"))
    first_pos = lax.axis_index("seq") * tokens_here
    carried = jnp.where(first_pos % seq_length != 0, 1.0, 0.0).astype(f32)
    inputs = hidden_in.astype(f32)
    scale_one = rms_scale(inputs)
    unit_one = inputs * scale_one
    normed_one = (unit_one * norm1_gain).astype(bf16)
    in_matrix = in_weight.reshape(features, 3 * channels)
    projected = jnp.dot(normed_one, in_matrix, preferred_element_type=f32)
    b_part = projected[:, :channels]
    c_part = projected[:, channels : 2 * channels]
    x_part = projected[:, 2 * channels :]
    gated = (b_part * x_part).astype(bf16)
    state = passed_along(gated[-2:], "seq", 1).astype(f32) * carried
    extended = jnp.concatenate([state, gated.astype(f32)], axis=0)
    convolved = (
        conv_weight[:, 0] * extended[:-2]
        + conv_weight[:, 1] * extended[1:-1]
        + conv_weight[:, 2] * extended[2:]
    )
    mixed = (c_part * convolved).astype(bf16)
    branch = lax.psum(jnp.dot(mixed, out_weight, preferred_element_type=f32), "head")
    middle = inputs + branch
    scale_two = rms_scale(middle)
    unit_two = middle * scale_two
    normed_two = (unit_two * norm2_gain).astype(bf16)
    gate_pre = jnp.dot(normed_two, gate_weight, preferred_element_type=f32)
    up_pre = jnp.dot(normed_two, up_weight, preferred_element_type=f32)
    sigmoid_gate = jax.nn.sigmoid(gate_pre)
    activated = gate_pre * sigmoid_gate
    hidden = (activated * up_pre).astype(bf16)
    ffn_out = lax.psum(
        jnp.dot(hidden, down_weight, preferred_element_type=f32).astype(jnp.bfloat16), "head"
    ).astype(jnp.float32)
    block_out = (middle + ffn_out).astype(bf16)
    cot_full = cotangent.astype(f32)
    down_grad = jnp.einsum("tf,td->fd", hidden, cotangent, preferred_element_type=f32)
    hidden_grad = jnp.einsum("td,fd->tf", cotangent, down_weight, preferred_element_type=f32)
    gate_grad = (
        hidden_grad * up_pre * sigmoid_gate * (1.0 + gate_pre * (1.0 - sigmoid_gate))
    ).astype(bf16)
    up_grad = (hidden_grad * activated).astype(bf16)
    gate_w_grad = jnp.einsum("td,tf->df", normed_two, gate_grad, preferred_element_type=f32)
    up_w_grad = jnp.einsum("td,tf->df", normed_two, up_grad, preferred_element_type=f32)
    normed_two_part = jnp.einsum("tf,df->td", gate_grad, gate_weight, preferred_element_type=f32)
    normed_two_part = normed_two_part + jnp.einsum(
        "tf,df->td", up_grad, up_weight, preferred_element_type=f32
    )
    normed_two_grad = lax.psum(normed_two_part.astype(jnp.bfloat16), "head").astype(jnp.float32)
    gain_two_grad = jnp.sum(normed_two_grad * unit_two, axis=0)
    middle_grad = cot_full + norm_back(normed_two_grad * norm2_gain, unit_two, scale_two)
    middle_low = middle_grad.astype(bf16)
    out_w_grad = jnp.einsum("tk,td->kd", mixed, middle_low, preferred_element_type=f32)
    mixed_grad = jnp.einsum("td,kd->tk", middle_low, out_weight, preferred_element_type=f32)
    c_grad = mixed_grad * convolved
    convolved_grad = mixed_grad * c_part
    conv_w_grad = jnp.stack(
        [jnp.sum(convolved_grad * extended[tap : tap + tokens_here], axis=0) for tap in range(3)],
        axis=1,
    )
    zero_pair = jnp.zeros((2, channels), f32)
    grad_padded = jnp.concatenate([zero_pair, convolved_grad, zero_pair], axis=0)
    extended_grad = (
        conv_weight[:, 0] * grad_padded[2:]
        + conv_weight[:, 1] * grad_padded[1:-1]
        + conv_weight[:, 2] * grad_padded[:-2]
    )
    sent_back = passed_along(extended_grad[:2] * carried, "seq", -1)
    gated_grad = extended_grad[2:] + jnp.concatenate(
        [jnp.zeros((tokens_here - 2, channels), f32), sent_back], axis=0
    )
    projected_grad = jnp.concatenate(
        [gated_grad * x_part, c_grad, gated_grad * b_part], axis=1
    ).astype(bf16)
    in_w_grad = jnp.einsum(
        "td,tc->dc", normed_one, projected_grad, preferred_element_type=f32
    ).reshape(features, 3, channels)
    normed_one_part = jnp.einsum("tc,dc->td", projected_grad, in_matrix, preferred_element_type=f32)
    normed_one_grad = lax.psum(normed_one_part.astype(jnp.bfloat16), "head").astype(jnp.float32)
    gain_one_grad = jnp.sum(normed_one_grad * unit_one, axis=0)
    input_grad = (
        middle_grad + norm_back(normed_one_grad * norm1_gain, unit_one, scale_one)
    ).astype(bf16)
    reduced = (
        lax.psum_scatter(gain_one_grad, "seq", scatter_dimension=0, tiled=True),
        lax.psum_scatter(in_w_grad, "seq", scatter_dimension=0, tiled=True),
        lax.psum_scatter(conv_w_grad, "seq", scatter_dimension=0, tiled=True),
        lax.psum_scatter(out_w_grad, "seq", scatter_dimension=0, tiled=True),
        lax.psum_scatter(gain_two_grad, "seq", scatter_dimension=0, tiled=True),
        lax.psum_scatter(gate_w_grad, "seq", scatter_dimension=0, tiled=True),
        lax.psum_scatter(up_w_grad, "seq", scatter_dimension=0, tiled=True),
        lax.psum_scatter(down_grad, "seq", scatter_dimension=0, tiled=True),
    )
    (
        gain_one_final,
        in_final,
        conv_final,
        out_final,
        gain_two_final,
        gate_final,
        up_final,
        down_final,
    ) = reduced
    return (
        block_out,
        input_grad,
        gain_one_final,
        in_final,
        conv_final,
        out_final,
        gain_two_final,
        gate_final,
        up_final,
        down_final,
    )


def solution(mesh):
    placed = (
        P("seq", None),
        P(),
        P(None, None, "head"),
        P("head", None),
        P("head", None),
        P(),
        P(None, "head"),
        P(None, "head"),
        P("head", None),
        P("seq", None),
    )
    return jax.shard_map(
        shards,
        mesh=mesh,
        in_specs=placed,
        out_specs=(
            P("seq", None),
            P("seq", None),
            P("seq"),
            P("seq", None, "head"),
            P(("head", "seq"), None),
            P(("head", "seq"), None),
            P("seq"),
            P("seq", "head"),
            P("seq", "head"),
            P(("head", "seq"), None),
        ),
        check_vma=False,
    )
```

profile of v0, /device:TPU:0, one launch (start us, length us, event | category | flops | bytes accessed | tf_op | source)
XLA Modules:
  0.0 1179.1 jit_solution(7096227214275198581)
XLA Ops:
  7.2 1.3 fusion.20
  8.6 4.7 copy.24
  13.3 3.0 fusion.31
  16.3 1.2 copy-done.5
  17.4 0.1 fusion.35
  17.6 3.6 collective-permute-start
  21.2 1.2 collective-permute-done
  22.4 2.0 multiply_convert_fusion.7
  24.5 1.4 fusion.38
  25.9 0.0 all-reduce.18.cloned.1.call-start
  26.0 28.3 %all-reduce.16.cloned.1.call-done = f32[256,1024]{1,0:T(8,128)} async-done(((f32[256,1024]{1,0:T(8,128)}), f32[256,1024]{1,0:T(8,128)}) %all-reduce.16.cloned.1.call-update) | async-done | bytes 1048592 | tf_op jit(solution)/shard_map/psum | solution.py:64
  54.3 1.4 multiply_reduce_fusion
  55.8 0.2 multiply_convert_fusion.3
  56.0 3.9 fusion.40
  59.9 1.4 fusion.39
  61.4 3.4 multiply_convert_fusion
  64.8 1.4 fusion.41
  66.3 2.2 fusion.6
  68.6 25.7 %all-reduce.18.cloned.1.call-done = bf16[256,1024]{1,0:T(8,128)(2,1)} async-done(((bf16[256,1024]{1,0:T(8,128)(2,1)}), bf16[256,1024]{1,0:T(8,128)(2,1)}) %all-reduce.18.cloned.1.call-update) | async-done | bytes 524304 | tf_op jit(solution)/shard_map/psum | solution.py:91
  94.3 1.5 fusion.16
  95.8 1.7 fusion.15
  97.5 0.5 fusion.28
  98.1 0.3 multiply_reduce_fusion.3
  98.4 0.1 copy-done.3
  98.5 0.2 fusion.23
  98.7 1.5 collective-permute-start.1
  100.2 4.7 convolution_convert_fusion
  104.9 0.2 multiply_convert_fusion.6
  105.1 0.7 copy-done.18
  105.8 0.1 copy-done.19
  105.9 1.8 convolution_convert_fusion.1
  107.7 0.0 all-reduce.20.cloned.1.call-start
  107.8 4.8 fusion.25
  112.6 9.4 copy.26
  122.0 0.0 reduce-scatter.7.cloned.1.call-start
  122.0 1.2 copy-done.4
  123.2 1.8 fusion.26
  125.1 0.0 reduce-scatter.11.cloned.1.call-start
  125.1 6.4 fusion.43
  131.6 6.4 fusion.42
  138.0 1.0 copy-done.11
  139.0 6.4 fusion.44
  145.4 236.4 %fusion = f32[40,1024]{1,0:T(8,128)S(1)} fusion(f32[2304,1024]{1,0:T(8,128)} %fusion.44), kind=kCustom, calls=%all-reduce-scatter | all-reduce-scatter fusion | flops 2621441 | bytes 9601536
  381.8 1.3 collective-permute-start.7
  383.2 1.3 collective-permute-start.8
  384.5 1.3 collective-permute-start.6
  385.8 1.3 collective-permute-start.5
  387.1 1.3 collective-permute-start.4
  388.4 1.3 collective-permute-start.3
  389.7 2.0 collective-permute-start.2
  391.8 0.6 fusion.37
  394.4 0.2 collective-permute-done.2
  394.6 11.1 concatenate.25
  405.7 1.6 constant_dynamic-slice_fusion
  407.3 1.5 fusion.19
  408.8 347.8 %all-reduce.9 = (f32[1024]{0:T(1024)S(1)}, f32[512,3]{0,1:T(4,128)S(1)}, f32[1024]{0:T(1024)S(1)}) all-reduce(f32[1024]{0:T(1024)S(1)} %get-tuple-element.34, f32[512,3]{0,1:T(4,128)S(1)} %pad_maximum_fusion.6, f32[1024]{0:T(1024)S(1)} %get-tuple-element.30), channel_id=2, replica_groups=mesh['seq'=64,'head'=2] {'seq'}, use_global_device_ids=true, to_apply=%region_9.10.clone | all-reduce | flops 3584 | bytes 28672
  756.7 0.6 dynamic-slice.1
  757.2 0.6 dynamic-slice.7
  757.8 0.6 constant_dynamic-slice_fusion.1
  758.5 2.9 fusion.12
  761.4 0.9 constant_dynamic-slice_fusion.2
  762.3 0.7 copy.27
  763.0 179.5 %reduce-scatter.11.cloned.1.call-done = f32[16,2304]{1,0:T(8,128)} async-done(((f32[1024,2304]{1,0:T(8,128)}), f32[16,2304]{1,0:T(8,128)}) %reduce-scatter.11.cloned.1.call-update) | async-done | bytes 147472 | tf_op jit(solution)/shard_map/reduce_scatter | solution.py:133
  942.5 229.7 %reduce-scatter.9.cloned.1.call-done = f32[16,2304]{1,0:T(8,128)} async-done(((f32[1024,2304]{1,0:T(8,128)}), f32[16,2304]{1,0:T(8,128)}) %reduce-scatter.9.cloned.1.call-update) | async-done | bytes 147472 | tf_op jit(solution)/shard_map/reduce_scatter | solution.py:132
  (88 shorter events, 0.5 us)
Async XLA Ops:
  7.2 17.3 %copy-start = (bf16[512,1024]{1,0:T(8,128)(2,1)S(1)}, bf16[512,1024]{1,0:T(8,128)(2,1)}, u32[]{:S(2)}) copy-start(bf16[512,1024]{1,0:T(8,128)(2,1)} %param.14) | copy-start | bytes 3145732
  7.2 47.1 %all-reduce.16.cloned.1.call-start = ((), (), s32[]{:S(2)}) async-start(), calls=%async_computation.3 | async-start | bytes 2097152 | tf_op jit(solution)/shard_map/psum | solution.py:64
  8.5 4.7 copy-start.2
  8.6 4.7 copy-start.20
  13.3 7.9 copy-start.22
  16.3 1.2 copy-start.5
  17.5 8.4 copy-start.8
  17.5 8.4 copy-start.16
  17.6 4.9 collective-permute-start
  25.9 29.9 %copy-start.21 = (f32[1024]{0:T(1024)S(1)}, f32[1024]{0:T(1024)}, u32[]{:S(2)}) copy-start(f32[1024]{0:T(1024)} %param.15) | copy-start | bytes 12292
  25.9 68.4 %all-reduce.18.cloned.1.call-start = ((), (), s32[]{:S(2)}) async-start(), calls=%async_computation.4 | async-start | bytes 1048576 | tf_op jit(solution)/shard_map/psum | solution.py:91
  55.8 4.1 slice-start
  55.9 3.9 slice-start.1
  56.0 5.4 slice-start.4
  59.9 1.5 copy-start.10
  59.9 1.5 slice-start.5
  59.9 6.3 slice-start.2
  61.4 4.9 slice-start.3
  64.8 1.4 copy-start.14
  64.8 1.4 copy-start.15
  68.5 338.8 %all-reduce.22.cloned.1.call-start = ((), (), s32[]{:S(2)}) async-start(), calls=%async_computation.9 | async-start | bytes 2097152 | tf_op jit(solution)/shard_map/psum | solution.py:74
  95.8 2.2 copy-start.6
  95.8 2.2 copy-start.9
  95.8 2.2 copy-start.12
  95.8 2.2 copy-start.17
  97.5 1.0 copy-start.3
  98.0 2.1 copy-start.13
  98.7 6.2 collective-permute-start.1
  100.1 5.8 copy-start.7
  105.1 0.7 copy-start.18
  105.1 0.8 copy-start.19
  107.7 653.6 %all-reduce.20.cloned.1.call-start = ((), (), s32[]{:S(2)}) async-start(), calls=%async_computation.8 | async-start | bytes 16777216
  122.0 1.3 copy-start.4
  122.0 641.0 %reduce-scatter.7.cloned.1.call-start = ((), (), s32[]{:S(2)}) async-start(), calls=%async_computation.5 | async-start | bytes 2129920 | tf_op jit(solution)/shard_map/reduce_scatter | solution.py:130
  125.1 817.4 %reduce-scatter.11.cloned.1.call-start = ((), (), s32[]{:S(2)}) async-start(), calls=%async_computation.7 | async-start | bytes 9584640 | tf_op jit(solution)/shard_map/reduce_scatter | solution.py:133
  131.6 1040.7 %reduce-scatter.9.cloned.1.call-start = ((), (), s32[]{:S(2)}) async-start(), calls=%async_computation.6 | async-start | bytes 9584640 | tf_op jit(solution)/shard_map/reduce_scatter | solution.py:132
  138.0 1.0 copy-start.11
  145.4 246.4 %copy-start.23 = (u32[128]{0:T(128)S(1)}, u32[128]{0:T(128)}, u32[]{:S(2)}) copy-start(u32[128]{0:T(128)} %constant.45) | copy-start | bytes 1540
  381.8 7.9 collective-permute-start.7
  383.2 5.2 collective-permute-start.8
  384.5 9.9 collective-permute-start.6
  385.8 8.6 collective-permute-start.5
  387.1 7.3 collective-permute-start.4
  388.4 6.0 collective-permute-start.3
  389.7 4.9 collective-permute-start.2
  758.5 413.7 %copy-start.1 = (bf16[512,1024]{1,0:T(8,128)(2,1)S(1)}, bf16[512,1024]{1,0:T(8,128)(2,1)}, u32[]{:S(2)}) copy-start(bf16[512,1024]{1,0:T(8,128)(2,1)} %param.14) | copy-start | bytes 3145732
Sparse Core Ops, SparseCore 0:
  26.0 28.2 all-reduce.15
  68.6 25.6 all-reduce.17
  107.8 29.5 all-reduce.21
  143.5 216.6 all-reduce.19
  362.9 351.9 reduce-scatter.6
  720.6 221.8 reduce-scatter.10
  947.7 224.5 reduce-scatter.8
where the time goes:
time: 1180 us
  blocking collectives  584 us (49%)
  waiting for transfers between devices  465 us (39%)
  matrix products  49.5 us (4%)
  local copies, waits for them, and re-layouts  35.2 us (3%)
  between operations  16.7 us (1%)
  starting transfers between devices  15.2 us (1%)
  other arithmetic  13.3 us (1%)
    unnamed x2, blocking collectives  584 us
    reduce_scatter x1, waiting for transfers between devices, shards(): lax.psum_scatter(gate_w_grad, 'seq', scatter_dimension=0, tiled=True)  230 us
    reduce_scatter x1, waiting for transfers between devices, shards(): lax.psum_scatter(up_w_grad, 'seq', scatter_dimension=0, tiled=True)  180 us
    psum x1, waiting for transfers between devices, shards(): lax.psum(jnp.dot(mixed, out_weight, preferred_element_type=f32), 'head')  28.3 us
    unnamed x70, local copies, waits for them, and re-layouts  25.8 us
    psum x1, waiting for transfers between devices, shards(): lax.psum(normed_two_part.astype(jnp.bfloat16), 'head').astype(jnp.float32)  25.7 us
  transfers between devices with their start and end apart: 16, of which 6 were waited for; matrix products, arithmetic and copies ran while one was open for 25% of the time, Pallas kernels for 0%

commit v1 on v0

v1 whole, which is shorter than its diff:
```python
import functools
import jax
import jax.numpy as jnp
from jax import lax
from jax.experimental import pallas as pl
from jax.experimental.pallas import tpu as pltpu
from jax.sharding import PartitionSpec as P

EPS = 1e-05
SEQ_BASE = 4096
MESH = pl.DeviceIdType.MESH
F32 = jnp.float32
BF16 = jnp.bfloat16
NT = (((1,), (1,)), ((), ()))
N_SEMS = 170


class Place:
    def __init__(self):
        self.seq = lax.axis_index("seq")
        self.head = lax.axis_index("head")
        self.coord = {
            "z": lax.div(self.seq, 16),
            "x": lax.rem(lax.div(self.seq, 4), 4),
            "y": lax.rem(self.seq, 4),
        }

    def peer(self, axis, shift):
        moved = dict(self.coord)
        moved[axis] = lax.rem(moved[axis] + shift, 4)
        return ((moved["z"] * 4 + moved["x"]) * 4 + moved["y"], self.head)

    def sibling(self):
        return (self.seq, 1 - self.head)


class Links:
    def __init__(self, send_sem, recv_sem):
        self.send_sem = send_sem
        self.recv_sem = recv_sem
        self.used = 0
        self.open = []

    def send(self, src, dst, device):
        copy = pltpu.make_async_remote_copy(
            src_ref=src,
            dst_ref=dst,
            send_sem=self.send_sem.at[self.used],
            recv_sem=self.recv_sem.at[self.used],
            device_id=device,
            device_id_type=MESH,
        )
        self.used += 1
        copy.start()
        self.open.append(copy)
        return copy

    def close(self):
        for copy in self.open:
            copy.wait_send()


class Ring:
    def __init__(self, place, links, axis, view, first, second):
        self.place, self.links, self.axis, self.view = place, links, axis, view
        self.first, self.second = first, second
        self.me = place.coord[axis]

    def block(self, shift):
        return lax.rem(self.me + shift, 4)

    def start(self):
        right, left = self.place.peer(self.axis, 1), self.place.peer(self.axis, 3)
        send = self.links.send
        self.far = [
            send(self.view(self.block(2), 0), self.first.at[0], right),
            send(self.view(self.block(2), 1), self.first.at[1], left),
        ]
        self.near = [
            send(self.view(self.block(1), 1), self.second.at[0, 1], right),
            send(self.view(self.block(3), 0), self.second.at[1, 0], left),
        ]

    def pass_on(self):
        right, left = self.place.peer(self.axis, 1), self.place.peer(self.axis, 3)
        for half, shift, device in ((0, 1, right), (1, 3, left)):
            self.far[half].wait_recv()
            own = self.view(self.block(shift), half)
            own[...] = (own[...].astype(F32) + self.first[half].astype(F32)).astype(BF16)
            self.near.append(self.links.send(own, self.second.at[half, half], device))

    def total(self, half):
        if half == 0:
            for copy in self.near:
                copy.wait_recv()
        own = self.view(self.block(0), half)[...].astype(F32)
        return own + self.second[0, half].astype(F32) + self.second[1, half].astype(F32)


def halves_of(ref, axis_dim, half_dim):
    extent = ref.shape[half_dim] // 2

    def view(block, half):
        index = [slice(None)] * len(ref.shape)
        index[half_dim] = pl.ds(half * extent, extent)
        index[axis_dim] = block
        return ref.at[tuple(index)]

    return view


def grads_kernel(
    n1t, n2t, hidt, gatet, upt, pgrad, mixedt, mlow, cot, small,
    gate_out, up_out, down_out, in_out, out_out, small_out,
    n2x, n2y, cotz, gx, uy, hz,
    g1, g1a, g1b, g2, g2a, g2b, ga,
    u1, u1a, u1b, u2, u2a, u2b, ua,
    d1, d1a, d1b, dt, d2, d2a, d2b,
    ia, ia1, ia2, ib, ib1, ib2, ic, ic1, ic2,
    oa, oa1, oa2, ob, ob1, ob2, oc, oc1, oc2,
    sm1, sm2,
    send_sem, recv_sem,
):
    place = Place()
    links = Links(send_sem, recv_sem)
    barrier = pltpu.get_barrier_semaphore()
    peers = [place.peer(axis, shift) for axis in "zxy" for shift in (1, 2, 3)]
    peers.append(place.sibling())
    for device in peers:
        pl.semaphore_signal(barrier, inc=1, device_id=device, device_id_type=MESH)
    pl.semaphore_wait(barrier, len(peers))
    head = place.head

    gathered = {}
    traded = {}
    for axis, src, dst in (("z", cot, cotz), ("x", n2t, n2x), ("y", n2t, n2y)):
        for shift in (1, 3, 2):
            gathered[axis, shift] = links.send(
                src.at[pl.ds(2 * head, 2)], dst.at[shift - 1, pl.ds(2 * head, 2)], place.peer(axis, shift)
            )
    for axis, src, dst in (("z", hidt, hz), ("x", gatet, gx), ("y", upt, uy)):
        for shift in (1, 3, 2):
            block = lax.rem(place.coord[axis] + shift, 4)
            traded[axis, shift] = links.send(src.at[block], dst.at[shift - 1], place.peer(axis, shift))

    small_links = [links.send(small, sm1.at[0, shift - 1], place.peer("z", shift)) for shift in (1, 3, 2)]

    in_rings = [
        Ring(place, links, "z", lambda b, h: ia.at[0, b, pl.ds(2 * h, 2)], ia1.at[0], ia2.at[0]),
        Ring(place, links, "x", lambda b, h: ia.at[1, pl.ds(2 * h, 2), b], ia1.at[1], ia2.at[1]),
        Ring(place, links, "y", lambda b, h: ia.at[2, pl.ds(2 * h, 2), :, b], ia1.at[2], ia2.at[2]),
    ]
    for part in range(3):
        def in_tile(i, carry, part=part):
            res = jnp.dot(n1t[i], pgrad[:, part * 512:(part + 1) * 512], preferred_element_type=F32)
            ia[part, i] = res.astype(BF16).reshape(4, 4, 16, 512)
            return carry

        lax.fori_loop(0, 4, in_tile, 0)
        in_rings[part].start()

    def out_tile(i, carry):
        res = jnp.dot(mixedt[i], mlow[...], preferred_element_type=F32)
        oa[i] = res.astype(BF16).reshape(8, 16, 1024)
        return carry

    lax.fori_loop(0, 4, out_tile, 0)
    out_ring = Ring(place, links, "z", halves_of(oa, 0, 1), oa1, oa2)
    out_ring.start()

    shared = {}
    for axis, dst in (("z", cotz), ("x", n2x), ("y", n2y)):
        for shift in (1, 3, 2):
            gathered[axis, shift].wait_recv()
            here = dst.at[shift - 1, pl.ds(2 * head, 2)]
            shared[axis, shift] = links.send(here, here, place.sibling())

    for ring in in_rings:
        ring.pass_on()
    out_ring.pass_on()

    for copy in small_links:
        copy.wait_recv()
    sm2[0] = small[...] + sm1[0, 0] + sm1[0, 1] + sm1[0, 2]
    small_links = [links.send(sm2.at[0], sm1.at[1, shift - 1], place.peer("x", shift)) for shift in (1, 3, 2)]

    def ready(axis):
        for shift in (1, 3, 2):
            shared[axis, shift].wait_recv()
            traded[axis, shift].wait_recv()

    def wide(own_x, got_x, own_g, got_g, me, store):
        def tile(i, carry):
            res = lax.dot_general(own_x[i], own_g[me], NT, preferred_element_type=F32)
            for d in range(3):
                res += lax.dot_general(got_x[d, i], got_g[d], NT, preferred_element_type=F32)
            store(i, res.astype(BF16))
            return carry

        lax.fori_loop(0, 4, tile, 0)

    ready("z")

    def down_tile(i, carry):
        res = jnp.dot(
            hidt[place.coord["z"], i], cot[...].reshape(256, 1024), preferred_element_type=F32
        )
        for d in range(3):
            res += jnp.dot(hz[d, i], cotz[d].reshape(256, 1024), preferred_element_type=F32)
        d1[i] = res.astype(BF16).reshape(9, 16, 1024)
        return carry

    lax.fori_loop(0, 4, down_tile, 0)
    down_ring = Ring(place, links, "x", halves_of(d1, 0, 3), d1a, d1b)
    down_ring.start()

    ready("x")

    def gate_store(i, res):
        g1[pl.ds(4 * i, 4)] = res.reshape(4, 4, 16, 576)

    wide(n2t, n2x, gatet, gx, place.coord["x"], gate_store)
    gate_ring = Ring(place, links, "y", halves_of(g1, 1, 0), g1a, g1b)
    gate_ring.start()

    ready("y")

    def up_store(i, res):
        u1[i] = res.reshape(16, 16, 576)

    wide(n2t, n2y, upt, uy, place.coord["y"], up_store)
    up_ring = Ring(place, links, "z", halves_of(u1, 0, 1), u1a, u1b)
    up_ring.start()

    for half in range(2):
        ib[0, pl.ds(2 * half, 2)] = in_rings[0].total(half).astype(BF16)
    for half in range(2):
        ib[1, pl.ds(2 * half, 2)] = in_rings[1].total(half).astype(BF16)
    for half in range(2):
        ib[2, pl.ds(2 * half, 2)] = in_rings[2].total(half).astype(BF16)
    in_rings = [
        Ring(place, links, "x", halves_of(ib.at[0], 0, 1), ib1.at[0], ib2.at[0]),
        Ring(place, links, "y", halves_of(ib.at[1], 1, 0), ib1.at[1], ib2.at[1]),
        Ring(place, links, "z", halves_of(ib.at[2], 0, 1), ib1.at[2], ib2.at[2]),
    ]
    for ring in in_rings:
        ring.start()
    for half in range(2):
        ob[pl.ds(2 * half, 2)] = out_ring.total(half).astype(BF16).reshape(2, 2, 16, 1024)
    out_ring = Ring(place, links, "x", halves_of(ob, 0, 1), ob1, ob2)
    out_ring.start()

    down_ring.pass_on()
    gate_ring.pass_on()
    up_ring.pass_on()
    for ring in in_rings:
        ring.pass_on()
    out_ring.pass_on()

    for copy in small_links:
        copy.wait_recv()
    sm2[1] = sm2[0] + sm1[1, 0] + sm1[1, 1] + sm1[1, 2]
    small_links = [links.send(sm2.at[1], sm1.at[2, shift - 1], place.peer("y", shift)) for shift in (1, 3, 2)]

    dt[pl.ds(144, 16), :] = jnp.zeros((16, 1024), F32)
    for half in range(2):
        dt[pl.ds(0, 144), half * 512:(half + 1) * 512] = down_ring.total(half).reshape(144, 512)
    for y in range(4):
        d2[y] = dt[pl.ds(36 * y, 48), :].astype(BF16)
    down_ring = Ring(place, links, "y", halves_of(d2, 0, 2), d2a, d2b)
    down_ring.start()
    for half in range(2):
        g2[pl.ds(2 * half, 2)] = gate_ring.total(half).astype(BF16).reshape(2, 4, 16, 576)
    gate_ring = Ring(place, links, "z", halves_of(g2, 0, 1), g2a, g2b)
    gate_ring.start()
    for half in range(2):
        u2[pl.ds(2 * half, 2)] = up_ring.total(half).astype(BF16).reshape(2, 4, 16, 576)
    up_ring = Ring(place, links, "x", halves_of(u2, 0, 1), u2a, u2b)
    up_ring.start()
    for part in range(3):
        for half in range(2):
            ic[part, pl.ds(2 * half, 2)] = in_rings[part].total(half).astype(BF16)
    in_rings = [
        Ring(place, links, axis, halves_of(ic.at[part], 0, 2), ic1.at[part], ic2.at[part])
        for part, axis in enumerate("yzx")
    ]
    for ring in in_rings:
        ring.start()
    for half in range(2):
        res = out_ring.total(half).reshape(16, 1024).astype(BF16)
        for y in range(2):
            oc[2 * half + y] = jnp.concatenate([res[8 * y:8 * y + 8]] * 2, axis=0)
    out_ring = Ring(place, links, "y", halves_of(oc, 0, 2), oc1, oc2)
    out_ring.start()

    gate_ring.pass_on()
    up_ring.pass_on()
    down_ring.pass_on()
    for ring in in_rings:
        ring.pass_on()
    out_ring.pass_on()

    trades = []
    for ring, axis, own in ((gate_ring, "x", ga), (up_ring, "y", ua)):
        for half in range(2):
            own[0, pl.ds(2 * half, 2)] = ring.total(half)
        for shift in (1, 3, 2):
            block = lax.rem(place.coord[axis] + shift, 4)
            trades.append(
                links.send(own.at[0, block], own.at[1, place.coord[axis]], place.peer(axis, shift))
            )
    for half in range(2):
        down_out[:, half * 512:(half + 1) * 512] = down_ring.total(half)[:36]
    for part in range(3):
        for half in range(2):
            in_out[part, :, half * 256:(half + 1) * 256] = in_rings[part].total(half)
    for half in range(2):
        out_out[:, half * 512:(half + 1) * 512] = out_ring.total(half)[:8]
    for copy in small_links:
        copy.wait_recv()
    small_out[...] = sm2[1] + sm1[2, 0] + sm1[2, 1] + sm1[2, 2]
    for copy in trades:
        copy.wait_recv()
    for own, axis, out in ((ga, "x", gate_out), (ua, "y", up_out)):
        me = place.coord[axis]
        own[1, me] = own[0, me]
        out[...] = jnp.concatenate([own[1, p] for p in range(4)], axis=1)
    links.close()


def weight_grads(n1t, n2t, hidt, gatet, upt, pgrad, mixedt, mlow, cot, small):
    v = lambda *shape: pltpu.VMEM(shape, BF16)
    f = lambda *shape: pltpu.VMEM(shape, F32)

    def ring(*half):
        return [v(2, *half), v(2, 2, *half)]

    scratch = [
        v(3, 4, 256, 256), v(3, 4, 256, 256), v(3, 4, 64, 1024),
        v(3, 576, 256), v(3, 576, 256), v(3, 4, 144, 256),
        v(16, 4, 16, 576), *ring(8, 16, 576), v(4, 4, 16, 576), *ring(2, 16, 576), f(2, 4, 16, 576),
        v(4, 16, 16, 576), *ring(8, 16, 576), v(4, 4, 16, 576), *ring(2, 16, 576), f(2, 4, 16, 576),
        v(4, 9, 16, 1024), *ring(9, 16, 512), f(160, 1024), v(4, 48, 1024), *ring(48, 512),
        v(3, 4, 4, 4, 16, 512), v(3, 2, 2, 4, 16, 512), v(3, 2, 2, 2, 4, 16, 512),
        v(3, 4, 4, 16, 512), v(3, 2, 2, 16, 512), v(3, 2, 2, 2, 16, 512),
        v(3, 4, 16, 512), v(3, 2, 16, 256), v(3, 2, 2, 16, 256),
        v(4, 8, 16, 1024), *ring(4, 16, 1024),
        v(4, 2, 16, 1024), *ring(1, 16, 1024),
        v(4, 16, 1024), *ring(16, 512),
        f(3, 3, 8, 1024), f(2, 8, 1024),
        pltpu.SemaphoreType.DMA((N_SEMS,)), pltpu.SemaphoreType.DMA((N_SEMS,)),
    ]
    vmem = pl.BlockSpec(memory_space=pltpu.VMEM)
    return pl.pallas_call(
        grads_kernel,
        out_shape=[
            jax.ShapeDtypeStruct(shape, F32)
            for shape in ((16, 2304), (16, 2304), (36, 1024), (3, 16, 512), (8, 1024), (8, 1024))
        ],
        in_specs=[vmem] * 10,
        out_specs=[vmem] * 6,
        scratch_shapes=scratch,
        compiler_params=pltpu.CompilerParams(
            collective_id=0, has_side_effects=True, vmem_limit_bytes=56 * 2**20
        ),
        name="weight_grads",
    )(
        n1t.reshape(4, 256, 256), n2t.reshape(4, 256, 256), hidt.reshape(4, 4, 144, 256),
        gatet.reshape(4, 576, 256), upt.reshape(4, 576, 256), pgrad, mixedt.reshape(4, 128, 256),
        mlow, cot.reshape(4, 64, 1024), small,
    )


def passed_along(value, axis, steps):
    count = lax.axis_size(axis)
    initial, last = (max(0, -steps), min(count, count - steps))
    return lax.ppermute(value, axis, [(source, source + steps) for source in range(initial, last)])


def from_other(value):
    return lax.ppermute(value, "head", [(0, 1), (1, 0)])


def rms_scale(values):
    return lax.rsqrt(jnp.mean(values * values, axis=-1, keepdims=True) + EPS)


def norm_back(unit_grad, unit, scale):
    return scale * (unit_grad - unit * jnp.mean(unit_grad * unit, axis=-1, keepdims=True))


def shards(
    hidden_in,
    norm1_gain,
    in_weight,
    conv_weight,
    out_weight,
    norm2_gain,
    gate_weight,
    up_weight,
    down_weight,
    cotangent,
):
    tokens_here = hidden_in.shape[0]
    features = hidden_in.shape[1]
    channels = in_weight.shape[2]
    f32 = jnp.float32
    bf16 = jnp.bfloat16
    seq_length = min(SEQ_BASE, tokens_here * lax.axis_size("seq"))
    place = lax.axis_index("seq")
    first_pos = place * tokens_here
    carried = jnp.where(first_pos % seq_length != 0, 1.0, 0.0).astype(f32)
    inputs = hidden_in.astype(f32)
    scale_one = rms_scale(inputs)
    unit_one = inputs * scale_one
    normed_one = (unit_one * norm1_gain).astype(bf16)
    in_matrix = in_weight.reshape(features, 3 * channels)
    projected = jnp.dot(normed_one, in_matrix, preferred_element_type=f32)
    b_part = projected[:, :channels]
    c_part = projected[:, channels : 2 * channels]
    x_part = projected[:, 2 * channels :]
    gated = (b_part * x_part).astype(bf16)
    state = passed_along(gated[-2:], "seq", 1).astype(f32) * carried
    extended = jnp.concatenate([state, gated.astype(f32)], axis=0)
    convolved = (
        conv_weight[:, 0] * extended[:-2]
        + conv_weight[:, 1] * extended[1:-1]
        + conv_weight[:, 2] * extended[2:]
    )
    mixed = (c_part * convolved).astype(bf16)
    branch = jnp.dot(mixed, out_weight, preferred_element_type=f32)
    branch = branch + from_other(branch)
    middle = inputs + branch
    scale_two = rms_scale(middle)
    unit_two = middle * scale_two
    normed_two = (unit_two * norm2_gain).astype(bf16)
    gate_pre = jnp.dot(normed_two, gate_weight, preferred_element_type=f32)
    up_pre = jnp.dot(normed_two, up_weight, preferred_element_type=f32)
    sigmoid_gate = jax.nn.sigmoid(gate_pre)
    activated = gate_pre * sigmoid_gate
    hidden = (activated * up_pre).astype(bf16)
    ffn_part = jnp.dot(hidden, down_weight, preferred_element_type=f32).astype(bf16)
    ffn_out = ffn_part.astype(f32) + from_other(ffn_part).astype(f32)
    block_out = (middle + ffn_out).astype(bf16)
    cot_full = cotangent.astype(f32)
    hidden_grad = jnp.einsum("td,fd->tf", cotangent, down_weight, preferred_element_type=f32)
    gate_grad = (
        hidden_grad * up_pre * sigmoid_gate * (1.0 + gate_pre * (1.0 - sigmoid_gate))
    ).astype(bf16)
    up_grad = (hidden_grad * activated).astype(bf16)
    normed_two_part = jnp.einsum("tf,df->td", gate_grad, gate_weight, preferred_element_type=f32)
    normed_two_part = normed_two_part + jnp.einsum(
        "tf,df->td", up_grad, up_weight, preferred_element_type=f32
    )
    normed_two_part = normed_two_part.astype(bf16)
    normed_two_grad = normed_two_part.astype(f32) + from_other(normed_two_part).astype(f32)
    gain_two_grad = jnp.sum(normed_two_grad * unit_two, axis=0)
    middle_grad = cot_full + norm_back(normed_two_grad * norm2_gain, unit_two, scale_two)
    middle_low = middle_grad.astype(bf16)
    mixed_grad = jnp.einsum("td,kd->tk", middle_low, out_weight, preferred_element_type=f32)
    c_grad = mixed_grad * convolved
    convolved_grad = mixed_grad * c_part
    conv_w_grad = [
        jnp.sum(convolved_grad * extended[tap : tap + tokens_here], axis=0) for tap in range(3)
    ]
    zero_pair = jnp.zeros((2, channels), f32)
    grad_padded = jnp.concatenate([zero_pair, convolved_grad, zero_pair], axis=0)
    extended_grad = (
        conv_weight[:, 0] * grad_padded[2:]
        + conv_weight[:, 1] * grad_padded[1:-1]
        + conv_weight[:, 2] * grad_padded[:-2]
    )
    sent_back = passed_along(extended_grad[:2] * carried, "seq", -1)
    gated_grad = extended_grad[2:] + jnp.concatenate(
        [jnp.zeros((tokens_here - 2, channels), f32), sent_back], axis=0
    )
    projected_grad = jnp.concatenate(
        [gated_grad * x_part, c_grad, gated_grad * b_part], axis=1
    ).astype(bf16)
    normed_one_part = jnp.einsum(
        "tc,dc->td", projected_grad, in_matrix, preferred_element_type=f32
    ).astype(bf16)
    normed_one_grad = normed_one_part.astype(f32) + from_other(normed_one_part).astype(f32)
    gain_one_grad = jnp.sum(normed_one_grad * unit_one, axis=0)
    input_grad = (
        middle_grad + norm_back(normed_one_grad * norm1_gain, unit_one, scale_one)
    ).astype(bf16)
    pad = jnp.zeros((features - channels,), f32)
    empty = jnp.zeros((features,), f32)
    small = jnp.stack(
        [gain_one_grad, gain_two_grad]
        + [jnp.concatenate([tap, pad]) for tap in conv_w_grad]
        + [empty] * 3
    )
    gate_final, up_final, down_final, in_final, out_final, small_final = weight_grads(
        normed_one.T, normed_two.T, hidden.T, gate_grad.T, up_grad.T,
        projected_grad, mixed.T, middle_low, cotangent, small,
    )
    gains = lax.dynamic_slice(small_final, (0, place * 16), (2, 16))
    conv_final = lax.dynamic_slice(small_final, (2, place * 8), (3, 8)).T
    return (
        block_out,
        input_grad,
        gains[0],
        in_final.transpose(1, 0, 2),
        conv_final,
        out_final,
        gains[1],
        gate_final,
        up_final,
        down_final,
    )


def solution(mesh):
    placed = (
        P("seq", None),
        P(),
        P(None, None, "head"),
        P("head", None),
        P("head", None),
        P(),
        P(None, "head"),
        P(None, "head"),
        P("head", None),
        P("seq", None),
    )
    return jax.shard_map(
        shards,
        mesh=mesh,
        in_specs=placed,
        out_specs=(
            P("seq", None),
            P("seq", None),
            P("seq"),
            P("seq", None, "head"),
            P(("head", "seq"), None),
            P(("head", "seq"), None),
            P("seq"),
            P("seq", "head"),
            P("seq", "head"),
            P(("head", "seq"), None),
        ),
        check_vma=False,
    )
```

time: 1180 us -> 169 us (0.14)
  blocking collectives: 584 us -> 0 us
  waiting for transfers between devices: 465 us -> 9.15 us
  Pallas kernels: 0 us -> 85.5 us
  matrix products: 49.5 us -> 25.3 us
  between operations: 16.7 us -> 1.11 us
    unnamed x2 -> x0, blocking collectives: 584 us -> none
    reduce_scatter x3 -> x0, waiting for transfers between devices: 409 us -> none  [the longest x1 230 us: shards(): lax.psum_scatter(gate_w_grad, 'seq', scatter_dimension=0, tiled=True)]
    pallas_call x0 -> x1, Pallas kernels: none -> 85.5 us  [weight_grads(): pl.pallas_call(grads_kernel, out_shape=[jax.ShapeDtypeStruct(shape, F32)...]
    psum x3 -> x0, waiting for transfers between devices: 54.1 us -> none  [the longest x1 28.3 us: shards(): lax.psum(jnp.dot(mixed, out_weight, preferred_element_type=f32), 'head')]
    dot_general x7 -> x2, matrix products: 31.9 us -> 5.18 us  [the longest x1 4.75 us: shards(): jnp.dot(hidden, down_weight, preferred_element_type=f32).astype(bf16)]
    unnamed x70, local copies, waits for them, and re-layouts: 25.8 us -> 10.8 us
  transfers between devices with their start and end apart: 16 -> 6, of which waited for: 6 -> 4; matrix products, arithmetic and copies ran while one was open for 25% -> 15% of each run, Pallas kernels for 0% -> 51%
where the time goes in v1:
time: 169 us
  Pallas kernels  85.5 us (51%)
  local copies, waits for them, and re-layouts  26.1 us (15%)
  matrix products  25.3 us (15%)
  other arithmetic  15.8 us (9%)
  waiting for transfers between devices  9.15 us (5%)
  starting transfers between devices  5.78 us (3%)
    pallas_call x1, Pallas kernels, weight_grads(): pl.pallas_call(grads_kernel, out_shape=[jax.ShapeDtypeStruct(shape, F32)...  85.5 us
    unnamed x70, local copies, waits for them, and re-layouts  10.8 us
    ppermute x2, starting transfers between devices, passed_along(): lax.ppermute(value, axis, [(source, source + steps) for source in range(i...  5.03 us
    dot_general x1, matrix products, shards(): jnp.dot(hidden, down_weight, preferred_element_type=f32).astype(bf16)  4.75 us
    ppermute x2, waiting for transfers between devices, passed_along(): lax.ppermute(value, axis, [(source, source + steps) for source in range(i...  4.7 us
    ppermute x4, waiting for transfers between devices, from_other(): return lax.ppermute(value, 'head', [(0, 1), (1, 0)])  4.45 us
    dot_general x1, matrix products, shards(): jnp.einsum('td,fd->tf', cotangent, down_weight, preferred_element_type=f32)  4.34 us
    dot_general x1, matrix products, shards(): jnp.einsum('tc,dc->td', projected_grad, in_matrix, preferred_element_type...  3.91 us
  transfers between devices with their start and end apart: 6, of which 4 were waited for; matrix products, arithmetic and copies ran while one was open for 15% of the time, Pallas kernels for 51%

profile of v1, /device:TPU:0, one launch (start us, length us, event | category | flops | bytes accessed | tf_op | source)
XLA Modules:
  0.0 168.6 jit_solution(832793713620125136)
XLA Ops:
  0.6 0.0 copy-start
  0.7 1.3 fusion.23
  2.0 0.0 copy-start.2
  2.0 0.0 copy-start.23
  2.0 4.7 %copy.26 = bf16[1024,3,512]{0,2,1:T(8,128)(2,1)} copy(bf16[1024,3,512]{2,0,1:T(8,128)(2,1)} %param.12) | data formatting | bytes 6291456 | tf_op args[2]
  6.7 0.0 slice-start.2
  6.7 3.0 %fusion.33 = f32[256,1536]{1,0:T(8,128)S(1)} fusion(bf16[1024,1536]{0,1:T(8,128)(2,1)} %bitcast.81, bf16[256,1024]{1,0:T(8,128)(2,1)S(1)} %copy-done.2, f32[1024]{0:T(1024)S(1)} %copy-done.23, f32[256]{0:T(256)S(1)} %add_rsqrt_fusion.1), kind=kOutput, calls=%fused_computation.72 | convolution fusion | flops 806354944 | bytes 5248000 | tf_op jit(solution)/shard_map/dot_general | solution.py:418
  9.7 1.2 copy-done.1
  11.0 0.1 fusion.39
  11.1 0.0 copy-start.8
  11.1 3.6 %collective-permute-start = (bf16[2,512]{1,0:T(2,128)(2,1)S(1)}, bf16[2,512]{1,0:T(2,128)(2,1)S(1)}, u32[]{:S(2)}, u32[]{:S(2)}) collective-permute-start(bf16[2,512]{1,0:T(2,128)(2,1)S(1)} %slice.68), channel_id=1, source_target_pairs={{0,2},{2,4},{4,6},{6,8},{8,10},{10,12},{12,14},{14,16},{16,18},{18... | collective-permute-start | bytes 6152 | tf_op jit(solution)/shard_map/ppermute | solution.py:377
  14.7 1.2 collective-permute-done
  16.0 1.4 multiply_convert_fusion.10
  17.4 0.4 fusion.41
  17.8 0.0 copy-start.21
  17.8 0.1 collective-permute-start.1
  17.9 2.6 %collective-permute-done.1 = f32[256,1024]{1,0:T(8,128)S(1)} collective-permute-done((f32[256,1024]{1,0:T(8,128)S(1)}, f32[256,1024]{1,0:T(8,128)S(1)}, u32[]{:S(2)}, u32[]{:S(2)}) %collective-permute-start.1) | collective-permute-done | bytes 1048608 | tf_op jit(solution)/shard_map/ppermute | solution.py:381
  20.6 0.3 multiply_reduce_fusion.2
  20.9 0.0 slice-start.1
  20.9 0.0 slice-start.4
  20.9 1.4 fusion.43
  22.4 0.4 slice-done
  22.8 0.2 slice-done.1
  23.0 1.4 fusion.42
  24.4 0.4 slice-done.4
  24.8 0.3 copy-done.3
  25.1 0.2 slice-done.5
  25.3 4.3 %fusion.3 = (bf16[2304,256]{0,1:T(8,128)(2,1)}, bf16[2304,256]{0,1:T(8,128)(2,1)}, bf16[2304,256]{0,1:T(8,128)(2,1)}, f32[256,2304]{1,0:T(8,128)S(1)}) fusion(f32[256,2304]{1,0:T(8,128)S(1)} %fusion.42, f32[256,2304]{1,0:T(8,128)S(1)} %fusion.43, bf16[256,1024]{1,0:T(8,128)(2,1)S(1)} %copy-done.3, bf16[2304,1024]{1,0:T(8,128)(2,1)S(1)} %bitcast.108), kind=kOutput, calls=%fused_computation.5 | convolution fusion | flops 1216806912 | bytes 15859712 | tf_op jit(solution)/shard_map/td,fd->tf/dot_general | solution.py:446
  29.6 1.8 %fusion.15 = f32[256,1024]{1,0:T(8,128)S(1)} fusion(bf16[1024,2304]{1,0:T(8,128)(2,1)S(1)} %bitcast.87, f32[256,2304]{1,0:T(8,128)S(1)} %fusion.42, f32[256,2304]{1,0:T(8,128)S(1)} %get-tuple-element.50, f32[256,2304]{1,0:T(8,128)S(1)} %fusion.43), kind=kOutput, calls=%fused_computation.31 | convolution fusion | flops 1213857792 | bytes 12845056 | tf_op jit(solution)/shard_map/tf,df->td/dot_general | solution.py:451
  31.4 1.6 fusion.14
  33.0 0.0 copy-start.15
  33.0 0.2 collective-permute-start.3
  33.2 1.8 %collective-permute-done.3 = bf16[256,1024]{1,0:T(8,128)(2,1)S(1)} collective-permute-done((bf16[256,1024]{1,0:T(8,128)(2,1)S(1)}, bf16[256,1024]{1,0:T(8,128)(2,1)S(1)}, u32[]{:S(2)}, u32[]{:S(2)}) %collective-permute-start.3) | collective-permute-done | bytes 524320 | tf_op jit(solution)/shard_map/ppermute | solution.py:381
  35.0 0.4 multiply_reduce_fusion
  35.5 0.4 fusion.38.mlow
  35.9 2.6 %multiply_reduce_fusion.4 = (f32[512]{0:T(512)S(1)}, f32[512]{0:T(512)S(1)}, f32[512]{0:T(512)S(1)}, f32[256,512]{1,0:T(8,128)S(1)}, bf16[256,512]{1,0:T(8,128)(2,1)}) fusion(f32[256,512]{1,0:T(8,128)S(1)} %copy-done.9, f32[2,512]{1,0:T(2,128)S(1)} %convert_multiply_fusion.2, bf16[256,512]{1,0:T(8,128)(2,1)S(1)} %copy-done.15, f32[256,1536]{1,0:T(8,128)} %copy-done.1, ...), kind=kOutput, calls=%fused_computation.62 | convolution fusion | flops 270006784 | bytes 4204544 | tf_op jit(solution)/shard_map/td,kd->tk/dot_general | solution.py:460
  38.5 1.0 fusion.28
  39.5 0.7 slice_multiply_fusion.1
  40.2 1.5 collective-permute-start.4
  41.7 0.8 copy.30
  42.5 3.5 %collective-permute-done.4 = f32[2,512]{1,0:T(2,128)S(1)} collective-permute-done((f32[2,512]{1,0:T(2,128)S(1)}, f32[2,512]{1,0:T(2,128)S(1)}, u32[]{:S(2)}, u32[]{:S(2)}) %collective-permute-start.4) | collective-permute-done | bytes 4128 | tf_op jit(solution)/shard_map/ppermute | solution.py:377
  46.0 1.6 multiply_convert_fusion.9
  47.5 3.9 %convolution_convert_fusion.1 = bf16[256,1024]{1,0:T(8,128)(2,1)} fusion(bf16[1024,1536]{0,1:T(8,128)(2,1)} %bitcast.82, bf16[256,512]{1,0:T(8,128)(2,1)S(1)} %get-tuple-element.40, bf16[256,512]{1,0:T(8,128)(2,1)} %get-tuple-element.44, bf16[256,512]{1,0:T(8,128)(2,1)S(1)} %get-tuple-element.39), kind=kOutput, calls=%fused_computation.30 | convolution fusion | flops 807927808 | bytes 4456448 | tf_op jit(solution)/shard_map/tc,dc->td/dot_general | solution.py:480
  51.5 4.7 %convolution_convert_fusion = bf16[256,1024]{1,0:T(8,128)(2,1)} fusion(bf16[2304,1024]{1,0:T(8,128)(2,1)} %param.18, f32[256,2304]{1,0:T(8,128)S(1)} %copy-done.11, f32[256,2304]{1,0:T(8,128)S(1)} %copy-done.13), kind=kOutput, calls=%fused_computation.28 | convolution fusion | flops 1211760640 | bytes 9961472 | tf_op jit(solution)/shard_map/dot_general | solution.py:442
  56.2 2.4 %copy.27 = bf16[2304,256]{1,0:T(8,128)(2,1)} copy(bf16[2304,256]{0,1:T(8,128)(2,1)} %get-tuple-element.38) | data formatting | bytes 2359296 | tf_op jit(solution)/shard_map/convert_element_type | solution.py:441
  58.6 2.4 %copy.28 = bf16[2304,256]{1,0:T(8,128)(2,1)} copy(bf16[2304,256]{0,1:T(8,128)(2,1)} %get-tuple-element.37) | data formatting | bytes 2359296 | tf_op jit(solution)/shard_map/convert_element_type | solution.py:449
  61.0 2.4 %copy.29 = bf16[2304,256]{1,0:T(8,128)(2,1)} copy(bf16[2304,256]{0,1:T(8,128)(2,1)} %get-tuple-element.36) | data formatting | bytes 2359296 | tf_op jit(solution)/shard_map/convert_element_type | solution.py:450
  63.3 0.9 fusion.59
  64.3 2.0 %copy.34 = bf16[1024,256]{1,0:T(8,128)(2,1)} copy(bf16[1024,256]{0,1:T(8,128)(2,1)} %fusion.59) | data formatting | bytes 1048576 | tf_op jit(solution)/shard_map/reshape | solution.py:368
  66.3 0.5 collective-permute-start.2
  66.8 2.0 %pad_maximum_fusion.pgrad = bf16[256,1536]{1,0:T(8,128)(2,1)} fusion(bf16[256,512]{1,0:T(8,128)(2,1)} %copy-done.16, bf16[256,512]{1,0:T(8,128)(2,1)} %get-tuple-element.44, bf16[256,512]{1,0:T(8,128)(2,1)S(1)} %get-tuple-element.39), kind=kLoop, calls=%fused_computation.50 | loop fusion | flops 2359296 | bytes 1572864 | tf_op jit(solution)/shard_map/concatenate | solution.py:477
  68.8 2.5 %fusion.22 = (f32[1024]{0:T(1024)S(1)}, f32[256]{0:T(256)S(1)}, bf16[1024,256]{0,1:T(8,128)(2,1)}) fusion(bf16[256,1024]{1,0:T(8,128)(2,1)S(1)} %copy-done.2, bf16[256,1024]{1,0:T(8,128)(2,1)} %collective-permute-done.5, bf16[256,1024]{1,0:T(8,128)(2,1)} %convolution_convert_fusion.1, f32[256]{0:T(256)S(1)} %add_rsqrt_fusion.1, f32[1024]{0:T(1024)S(1)} %copy-done.23), kind=kLoop, calls=%fused_computation.38 | loop fusion | flops 3144448 | bytes 2107392 | tf_op jit(solution)/shard_map/reduce_sum | solution.py:484
  71.3 2.1 %copy.33 = bf16[1024,256]{1,0:T(8,128)(2,1)} copy(bf16[1024,256]{0,1:T(8,128)(2,1)} %get-tuple-element.43) | data formatting | bytes 1048576 | tf_op jit(solution)/shard_map/reshape | solution.py:368
  73.3 0.7 stack.27.small
  74.0 85.5 %weight_grads.1 = (f32[16,2304]{1,0:T(8,128)}, f32[16,2304]{1,0:T(8,128)}, f32[36,1024]{1,0:T(8,128)}, f32[3,16,512]{2,1,0:T(8,128)}, f32[8,1024]{1,0:T(8,128)}, /*index=5*/f32[8,1024]{1,0:T(8,128)}) custom-call(bf16[4,256,256]{2,1,0:T(8,128)(2,1)} %bitcast.93, bf16[4,256,256]{2,1,0:T(8,128)(2,1)} %bitcast.92, bf16[4,4,144,256]{3,2,1,0:T(8,128)(2,1)} %bitcast.83, ...), custom_call_target="tpu_custom_call" | custom-call | tf_op jit(solution)/shard_map/weight_grads/pallas_call | solution.py:354
  159.5 1.3 dynamic-slice_bitcast_fusion
  160.8 0.8 constant_dynamic-slice_fusion
  161.6 0.5 slice_bitcast_fusion
  162.2 3.2 %fusion.21 = (bf16[256,1024]{1,0:T(8,128)(2,1)}, bf16[256,1024]{1,0:T(8,128)(2,1)}) fusion(bf16[256,1024]{1,0:T(8,128)(2,1)S(1)} %copy-done.2, bf16[256,1024]{1,0:T(8,128)(2,1)} %collective-permute-done.5, bf16[256,1024]{1,0:T(8,128)(2,1)} %convolution_convert_fusion.1, f32[256]{0:T(256)S(1)} %broadcast_multiply_fusion, f32[1024]{0:T(1024)S(1)} %copy-done.23, ...), kind=kLoop, calls=%fused_computation.37 | loop fusion | flops 6815744 | bytes 6303744 | tf_op jit(solution)/shard_map/convert_element_type | solution.py:487
  165.4 0.6 copy.40
  166.0 0.6 copy.41
  166.6 0.7 copy.42
  167.3 0.7 copy.43
  168.0 0.7 copy.44
  (68 shorter events, 0.2 us)
Async XLA Ops:
  0.6 16.7 %copy-start = (bf16[512,1024]{1,0:T(8,128)(2,1)S(1)}, bf16[512,1024]{1,0:T(8,128)(2,1)}, u32[]{:S(2)}) copy-start(bf16[512,1024]{1,0:T(8,128)(2,1)} %param.14) | copy-start | bytes 3145732
  2.0 4.7 %copy-start.2 = (bf16[256,1024]{1,0:T(8,128)(2,1)S(1)}, bf16[256,1024]{1,0:T(8,128)(2,1)}, u32[]{:S(2)}) copy-start(bf16[256,1024]{1,0:T(8,128)(2,1)} %param.10) | copy-start | bytes 1572868
  2.0 4.7 %copy-start.23 = (f32[1024]{0:T(1024)S(1)}, f32[1024]{0:T(1024)}, u32[]{:S(2)}) copy-start(f32[1024]{0:T(1024)} %param.11) | copy-start | bytes 12292
  6.7 8.0 %copy-start.25 = (f32[512,3]{0,1:T(4,128)S(1)}, f32[512,3]{0,1:T(4,128)}, u32[]{:S(2)}) copy-start(f32[512,3]{0,1:T(4,128)} %param.13) | copy-start | bytes 18436
  6.7 14.2 %slice-start.2 = ((s8[4718592]{0:T(1024)(128)(4,1)}), s8[524288]{0:T(1024)(128)(4,1)S(1)}, s32[]{:S(2)}) async-start(s8[4718592]{0:T(1024)(128)(4,1)} %bitcast.88), calls=%async_computation.2 | async-start | bytes 1048576
  9.7 1.3 copy-start.1
  11.1 6.9 %copy-start.8 = (f32[256,512]{1,0:T(8,128)}, f32[256,512]{1,0:T(8,128)S(1)}, u32[]{:S(2)}) copy-start(f32[256,512]{1,0:T(8,128)S(1)} %get-tuple-element.34) | copy-start | bytes 1572868
  11.1 6.8 %copy-start.14 = (bf16[256,512]{1,0:T(8,128)(2,1)}, bf16[256,512]{1,0:T(8,128)(2,1)S(1)}, u32[]{:S(2)}) copy-start(bf16[256,512]{1,0:T(8,128)(2,1)S(1)} %get-tuple-element.35) | copy-start | bytes 786436
  11.1 4.9 %collective-permute-start = (bf16[2,512]{1,0:T(2,128)(2,1)S(1)}, bf16[2,512]{1,0:T(2,128)(2,1)S(1)}, u32[]{:S(2)}, u32[]{:S(2)}) collective-permute-start(bf16[2,512]{1,0:T(2,128)(2,1)S(1)} %slice.68), channel_id=1, source_target_pairs={{0,2},{2,4},{4,6},{6,8},{8,10},{10,12},{12,14},{14,16},{16,18},{18... | collective-permute-start | bytes 6152 | tf_op jit(solution)/shard_map/ppermute | solution.py:377
  16.0 4.9 %slice-start.3 = ((s8[4718592]{0:T(1024)(128)(4,1)}), s8[4194304]{0:T(1024)(128)(4,1)S(1)}, s32[]{:S(2)}) async-start(s8[4718592]{0:T(1024)(128)(4,1)} %bitcast.88), calls=%async_computation.3 | async-start | bytes 8388608
  17.8 3.1 %copy-start.21 = (f32[1024]{0:T(1024)S(1)}, f32[1024]{0:T(1024)}, u32[]{:S(2)}) copy-start(f32[1024]{0:T(1024)} %param.15) | copy-start | bytes 12292
  17.8 2.7 %collective-permute-start.1 = (f32[256,1024]{1,0:T(8,128)S(1)}, f32[256,1024]{1,0:T(8,128)S(1)}, u32[]{:S(2)}, u32[]{:S(2)}) collective-permute-start(f32[256,1024]{1,0:T(8,128)S(1)} %fusion.41), channel_id=1, source_target_pairs={{0,1},{1,0},{2,3},{3,2},{4,5},{5,4},{6,7},{7,6},{8,9},{9,8},{10,11... | collective-permute-start | bytes 3145736 | tf_op jit(solution)/shard_map/ppermute | solution.py:381
  20.6 2.2 %slice-start = ((s8[4718592]{0:T(1024)(128)(4,1)}), s8[4194304]{0:T(1024)(128)(4,1)S(1)}, s32[]{:S(2)}) async-start(s8[4718592]{0:T(1024)(128)(4,1)} %bitcast.86), calls=%async_computation | async-start | bytes 8388608
  20.9 2.0 %slice-start.1 = ((s8[4718592]{0:T(1024)(128)(4,1)}), s8[524288]{0:T(1024)(128)(4,1)S(1)}, s32[]{:S(2)}) async-start(s8[4718592]{0:T(1024)(128)(4,1)} %bitcast.86), calls=%async_computation.1 | async-start | bytes 1048576
  20.9 3.9 %slice-start.4 = ((s8[4718592]{0:T(1024)(128)(4,1)}), s8[4194304]{0:T(1024)(128)(4,1)S(1)}, s32[]{:S(2)}) async-start(s8[4718592]{0:T(1024)(128)(4,1)} %bitcast.107), calls=%async_computation.4 | async-start | bytes 8388608
  23.0 6.7 %copy-start.10 = (f32[256,2304]{1,0:T(8,128)}, f32[256,2304]{1,0:T(8,128)S(1)}, u32[]{:S(2)}) copy-start(f32[256,2304]{1,0:T(8,128)S(1)} %fusion.43) | copy-start | bytes 7077892
  23.0 2.2 %copy-start.3 = (bf16[256,1024]{1,0:T(8,128)(2,1)S(1)}, bf16[256,1024]{1,0:T(8,128)(2,1)}, u32[]{:S(2)}) copy-start(bf16[256,1024]{1,0:T(8,128)(2,1)} %param.19) | copy-start | bytes 1572868
  23.0 2.3 %slice-start.5 = ((s8[4718592]{0:T(1024)(128)(4,1)}), s8[524288]{0:T(1024)(128)(4,1)S(1)}, s32[]{:S(2)}) async-start(s8[4718592]{0:T(1024)(128)(4,1)} %bitcast.107), calls=%async_computation.5 | async-start | bytes 1048576
  25.3 6.1 %copy-start.12 = (f32[256,2304]{1,0:T(8,128)}, f32[256,2304]{1,0:T(8,128)S(1)}, u32[]{:S(2)}) copy-start(f32[256,2304]{1,0:T(8,128)S(1)} %fusion.42) | copy-start | bytes 7077892
  33.0 2.9 %copy-start.5 = (bf16[256,1024]{1,0:T(8,128)(2,1)}, bf16[256,1024]{1,0:T(8,128)(2,1)S(1)}, u32[]{:S(2)}) copy-start(bf16[256,1024]{1,0:T(8,128)(2,1)S(1)} %fusion.14) | copy-start | bytes 1572868
  33.0 2.9 %copy-start.9 = (f32[256,512]{1,0:T(8,128)S(1)}, f32[256,512]{1,0:T(8,128)}, u32[]{:S(2)}) copy-start(f32[256,512]{1,0:T(8,128)} %copy-done.8) | copy-start | bytes 1572868
  33.0 2.9 %copy-start.15 = (bf16[256,512]{1,0:T(8,128)(2,1)S(1)}, bf16[256,512]{1,0:T(8,128)(2,1)}, u32[]{:S(2)}) copy-start(bf16[256,512]{1,0:T(8,128)(2,1)} %copy-done.14) | copy-start | bytes 786436
  33.0 2.0 %collective-permute-start.3 = (bf16[256,1024]{1,0:T(8,128)(2,1)S(1)}, bf16[256,1024]{1,0:T(8,128)(2,1)S(1)}, u32[]{:S(2)}, u32[]{:S(2)}) collective-permute-start(bf16[256,1024]{1,0:T(8,128)(2,1)S(1)} %fusion.14), channel_id=1, source_target_pairs={{0,1},{1,0},{2,3},{3,2},{4,5},{5,4},{6,7},{7,6},{8,9},{9,8},{10,11... | collective-permute-start | bytes 1572872 | tf_op jit(solution)/shard_map/ppermute | solution.py:381
  35.9 3.6 %copy-start.7 = (bf16[256,1024]{1,0:T(8,128)(2,1)}, bf16[256,1024]{1,0:T(8,128)(2,1)S(1)}, u32[]{:S(2)}) copy-start(bf16[256,1024]{1,0:T(8,128)(2,1)S(1)} %fusion.38.mlow) | copy-start | bytes 1572868
  40.2 5.8 %collective-permute-start.4 = (f32[2,512]{1,0:T(2,128)S(1)}, f32[2,512]{1,0:T(2,128)S(1)}, u32[]{:S(2)}, u32[]{:S(2)}) collective-permute-start(f32[2,512]{1,0:T(2,128)S(1)} %slice_multiply_fusion.1), channel_id=1, source_target_pairs={{2,0},{4,2},{6,4},{8,6},{10,8},{12,10},{14,12},{16,14},{18,16},{20... | collective-permute-start | bytes 12296 | tf_op jit(solution)/shard_map/ppermute | solution.py:377
  47.5 3.9 %copy-start.16 = (bf16[256,512]{1,0:T(8,128)(2,1)}, bf16[256,512]{1,0:T(8,128)(2,1)S(1)}, u32[]{:S(2)}) copy-start(bf16[256,512]{1,0:T(8,128)(2,1)S(1)} %get-tuple-element.40) | copy-start | bytes 786436
  47.5 3.9 %copy-start.11 = (f32[256,2304]{1,0:T(8,128)S(1)}, f32[256,2304]{1,0:T(8,128)}, u32[]{:S(2)}) copy-start(f32[256,2304]{1,0:T(8,128)} %copy-done.10) | copy-start | bytes 7077892
  47.5 3.9 %copy-start.13 = (f32[256,2304]{1,0:T(8,128)S(1)}, f32[256,2304]{1,0:T(8,128)}, u32[]{:S(2)}) copy-start(f32[256,2304]{1,0:T(8,128)} %copy-done.12) | copy-start | bytes 7077892
  51.4 17.4 %collective-permute-start.5 = (bf16[256,1024]{1,0:T(8,128)(2,1)}, bf16[256,1024]{1,0:T(8,128)(2,1)}, u32[]{:S(2)}, u32[]{:S(2)}) collective-permute-start(bf16[256,1024]{1,0:T(8,128)(2,1)} %convolution_convert_fusion.1), channel_id=1, source_target_pairs={{0,1},{1,0},{2,3},{3,2},{4,5},{5,4},{6,7},{7,6},{8,9},{9,8},{10,11... | collective-permute-start | bytes 1572872 | tf_op jit(solution)/shard_map/ppermute | solution.py:381
  66.3 95.8 %collective-permute-start.2 = (bf16[256,1024]{1,0:T(8,128)(2,1)}, bf16[256,1024]{1,0:T(8,128)(2,1)}, u32[]{:S(2)}, u32[]{:S(2)}) collective-permute-start(bf16[256,1024]{1,0:T(8,128)(2,1)} %convolution_convert_fusion), channel_id=1, source_target_pairs={{0,1},{1,0},{2,3},{3,2},{4,5},{5,4},{6,7},{7,6},{8,9},{9,8},{10,11... | collective-permute-start | bytes 1572872 | tf_op jit(solution)/shard_map/ppermute | solution.py:381
  74.0 88.1 %copy-start.4 = (bf16[256,1024]{1,0:T(8,128)(2,1)S(1)}, bf16[256,1024]{1,0:T(8,128)(2,1)}, u32[]{:S(2)}) copy-start(bf16[256,1024]{1,0:T(8,128)(2,1)} %param.19) | copy-start | bytes 1572868
  74.0 88.1 %copy-start.6 = (bf16[256,1024]{1,0:T(8,128)(2,1)S(1)}, bf16[256,1024]{1,0:T(8,128)(2,1)}, u32[]{:S(2)}) copy-start(bf16[256,1024]{1,0:T(8,128)(2,1)} %copy-done.5) | copy-start | bytes 1572868
  74.0 88.2 %copy-start.17 = (bf16[256,1024]{1,0:T(8,128)(2,1)S(1)}, bf16[256,1024]{1,0:T(8,128)(2,1)}, u32[]{:S(2)}) copy-start(bf16[256,1024]{1,0:T(8,128)(2,1)} %convolution_convert_fusion) | copy-start | bytes 1572868
  162.1 3.3 %copy-start.22 = (f32[3,16,512]{2,1,0:T(8,128)S(1)}, f32[3,16,512]{2,1,0:T(8,128)}, u32[]{:S(2)}) copy-start(f32[3,16,512]{2,1,0:T(8,128)} %get-tuple-element.17) | copy-start | bytes 294916
  162.1 3.9 %copy-start.24 = (f32[8,1024]{1,0:T(8,128)S(1)}, f32[8,1024]{1,0:T(8,128)}, u32[]{:S(2)}) copy-start(f32[8,1024]{1,0:T(8,128)} %get-tuple-element.66) | copy-start | bytes 98308
  162.1 4.5 %copy-start.20 = (f32[16,2304]{1,0:T(8,128)S(1)}, f32[16,2304]{1,0:T(8,128)}, u32[]{:S(2)}) copy-start(f32[16,2304]{1,0:T(8,128)} %get-tuple-element.68) | copy-start | bytes 442372
  162.1 5.2 %copy-start.19 = (f32[16,2304]{1,0:T(8,128)S(1)}, f32[16,2304]{1,0:T(8,128)}, u32[]{:S(2)}) copy-start(f32[16,2304]{1,0:T(8,128)} %get-tuple-element.69) | copy-start | bytes 442372
  162.1 5.8 %copy-start.18 = (f32[36,1024]{1,0:T(8,128)S(1)}, f32[36,1024]{1,0:T(8,128)}, u32[]{:S(2)}) copy-start(f32[36,1024]{1,0:T(8,128)} %get-tuple-element.70) | copy-start | bytes 442372

commit v2 on v0

v2 whole, which is shorter than its diff:
```python
import jax
import jax.numpy as jnp
from jax import lax
from jax.experimental import pallas as pl
from jax.experimental.pallas import tpu as pltpu
from jax.sharding import PartitionSpec as P

EPS = 1e-05
MESH = pl.DeviceIdType.MESH
F32 = jnp.float32
BF16 = jnp.bfloat16
NT = (((1,), (1,)), ((), ()))
N_SEMS = 180
TILE = 768


class Place:
    def __init__(self):
        self.seq = lax.axis_index("seq")
        self.head = lax.axis_index("head")
        self.coord = {
            "z": lax.div(self.seq, 16),
            "x": lax.rem(lax.div(self.seq, 4), 4),
            "y": lax.rem(self.seq, 4),
        }

        self.blocks = {
            axis: [self.coord[axis]] + [lax.rem(self.coord[axis] + shift, 4) for shift in (1, 2, 3)]
            for axis in "zxy"
        }
        self.peers = {}
        for axis in "zxy":
            for shift in (1, 2, 3):
                moved = dict(self.coord)
                moved[axis] = self.blocks[axis][shift]
                self.peers[axis, shift] = ((moved["z"] * 4 + moved["x"]) * 4 + moved["y"], self.head)
        self.along = {
            shift: (lax.rem(self.seq + 64 + shift, 64), self.head) for shift in (1, -1)
        }

    def peer(self, axis, shift):
        return self.peers[axis, shift]

    def sibling(self):
        return (self.seq, 1 - self.head)


class Links:
    def __init__(self, send_sem, recv_sem):
        self.send_sem = send_sem
        self.recv_sem = recv_sem
        self.used = 0
        self.open = []

    def plan(self, src, dst, device):
        copy = pltpu.make_async_remote_copy(
            src_ref=src,
            dst_ref=dst,
            send_sem=self.send_sem.at[self.used],
            recv_sem=self.recv_sem.at[self.used],
            device_id=device,
            device_id_type=MESH,
        )
        self.used += 1
        return copy

    def send(self, src, dst, device):
        copy = self.plan(src, dst, device)
        copy.start()
        self.open.append(copy)
        return copy

    def close(self):
        for copy in self.open:
            copy.wait_send()
        self.open = []


class Ring:
    def __init__(self, place, links, axis, view, first, second):
        self.place, self.links, self.axis, self.view = place, links, axis, view
        self.first, self.second = first, second
        self.me = place.coord[axis]

    def block(self, shift):
        return self.place.blocks[self.axis][shift]

    def start(self):
        right, left = self.place.peer(self.axis, 1), self.place.peer(self.axis, 3)
        send = self.links.send
        self.far = [
            send(self.view(self.block(2), 0), self.first.at[0], right),
            send(self.view(self.block(2), 1), self.first.at[1], left),
        ]
        self.near = [
            send(self.view(self.block(1), 1), self.second.at[0, 1], right),
            send(self.view(self.block(3), 0), self.second.at[1, 0], left),
        ]

    def pass_on(self):
        right, left = self.place.peer(self.axis, 1), self.place.peer(self.axis, 3)
        for half, shift, device in ((0, 1, right), (1, 3, left)):
            self.far[half].wait_recv()
            own = self.view(self.block(shift), half)
            own[...] = (own[...].astype(F32) + self.first[half].astype(F32)).astype(BF16)
            self.near.append(self.links.send(own, self.second.at[half, half], device))

    def total(self, half):
        if half == 0:
            for copy in self.near:
                copy.wait_recv()
        own = self.view(self.block(0), half)[...].astype(F32)
        return own + self.second[0, half].astype(F32) + self.second[1, half].astype(F32)


def halves_of(ref, axis_dim, half_dim):
    extent = ref.shape[half_dim] // 2

    def view(block, half):
        index = [slice(None)] * len(ref.shape)
        index[half_dim] = pl.ds(half * extent, extent)
        index[axis_dim] = block
        return ref.at[tuple(index)]

    return view


def in_rows(extent, step, body, carry=0):
    def one(i, carry):
        return body(pl.multiple_of(i * step, step), carry)

    return lax.fori_loop(0, extent // step, one, carry)


def mean_square(values):
    return jnp.mean(values * values, axis=-1, keepdims=True)


def block_kernel(
    hin, gain1, w_in, w_conv, w_out, gain2, w_gate, w_up, w_down, cot,
    block_out, input_grad, gate_out, up_out, down_out, in_out, out_out, small_out,
    win, wout, n1, n1t, n2, n2t, hidt, gatet, upt, proj, gbuf, cv, mixed, mixedt, mid, mlow, cgbuf, mxg, pg,
    small, xb, xf, xn, xh,
    n2x, n2y, cotz, gx, uy, hz,
    g1a, g1b, g2a, g2b, ga,
    u1a, u1b, u2a, u2b, ua,
    d1a, d1b, d2a, d2b,
    ia1, ia2, ib1, ib2, ic1, ic2,
    oa1, oa2, ob1, ob2, oc1, oc2,
    sm1, sm2,
    send_sem, recv_sem, load_sem,
):
    place = Place()
    links = Links(send_sem, recv_sem)
    head = place.head
    barrier = pltpu.get_barrier_semaphore()
    peers = [place.peer(axis, shift) for axis in "zxy" for shift in (1, 2, 3)]
    peers += [place.sibling(), place.along[1], place.along[-1]]
    carried = jnp.where(lax.rem(place.seq, 16) != 0, 1.0, 0.0).astype(F32)
    carried_on = jnp.where(lax.rem(place.seq, 16) != 15, 1.0, 0.0).astype(F32)
    gathered = {}
    traded = {}
    shared = {}

    for axis, src, dst in (("z", cot, cotz), ("x", n2t, n2x), ("y", n2t, n2y)):
        part = src.shape[0] // 2
        mine = pl.ds(part * head, part)
        for shift in (1, 3, 2):
            gathered[axis, shift] = links.plan(
                src.at[mine], dst.at[shift - 1, mine], place.peer(axis, shift)
            )

    def gather(axis):
        for shift in (1, 3, 2):
            gathered[axis, shift].start()

    def trade(axis, src, dst):
        for shift in (1, 3, 2):
            block = place.blocks[axis][shift]
            rows = pl.ds(pl.multiple_of(block * 576, 576), 576)
            traded[axis, shift] = links.send(src.at[rows], dst.at[shift - 1], place.peer(axis, shift))

    def share(axis, dst):
        for shift in (1, 3, 2):
            gathered[axis, shift].wait_recv()
            part = dst.shape[1] // 2
            here = dst.at[shift - 1, pl.ds(part * head, part)]
            shared[axis, shift] = links.send(here, here, place.sibling())

    taps = w_conv[...]

    def shifted_gated(r):
        window = gbuf[pl.ds(r, 48), :].astype(F32)
        return [pltpu.roll(window, 2, 0)[16:], pltpu.roll(window, 1, 0)[16:], window[16:]]

    def forward(wg, wu, wd, pre_g, pre_u, grad_h, hid_s, gg_s, ug_s, ffn_acc, n2g_acc):
        loads = []
        for src, dst in (
            (w_in.at[0], win.at[0]), (w_in.at[1], win.at[1]), (w_in.at[2], win.at[2]),
            (w_out, wout), (w_gate, wg), (w_up, wu), (w_down, wd),
        ):
            copy = pltpu.make_async_copy(src, dst, load_sem.at[len(loads)])
            copy.start()
            loads.append(copy)
        for device in peers:
            pl.semaphore_signal(barrier, inc=1, device_id=device, device_id_type=MESH)

        def norm_one(r, carry):
            x = hin[pl.ds(r, 32), :].astype(F32)
            n1[pl.ds(r, 32), :] = (x * lax.rsqrt(mean_square(x) + EPS) * gain1[...]).astype(BF16)
            return carry

        in_rows(256, 32, norm_one)
        pl.semaphore_wait(barrier, len(peers))
        gather("z")
        for part in (0, 2, 1):
            loads[part].wait()
            proj[part] = jnp.dot(n1[...], win[part], preferred_element_type=F32)
            if part == 2:
                def gate_rows(r, carry):
                    here = pl.ds(r, 32)
                    gbuf[pl.ds(r + 16, 32), :] = (proj[0, here, :] * proj[2, here, :]).astype(BF16)
                    return carry

                in_rows(256, 32, gate_rows)
                edge = links.send(gbuf.at[pl.ds(256, 16)], gbuf.at[pl.ds(0, 16)], place.along[1])
        for i in range(4):
            n1t[i] = n1[:, 256 * i:256 * i + 256].T
        loads[3].wait()
        edge.wait_recv()
        gbuf[pl.ds(0, 16), :] = (gbuf[pl.ds(0, 16), :].astype(F32) * carried).astype(BF16)

        def mix_rows(r, carry):
            here = pl.ds(r, 32)
            old, last, now = shifted_gated(r)
            value = taps[0:1] * old + taps[1:2] * last + taps[2:3] * now
            cv[here, :] = value
            mixed[here, :] = (proj[1, here, :] * value).astype(BF16)
            return carry

        in_rows(256, 32, mix_rows)
        branch = []
        for half in range(2):
            here = pl.ds(128 * half, 128)
            xb[0, here, :] = jnp.dot(mixed[here, :], wout[...], preferred_element_type=F32).astype(BF16)
            branch.append(links.send(xb.at[0, here], xb.at[1, here], place.sibling()))
        for i in range(4):
            mixedt[i] = mixed[:, 128 * i:128 * i + 128].T

        def norm_two(r, carry):
            here = pl.ds(r, 32)
            middle = hin[here, :].astype(F32) + (xb[0, here, :].astype(F32) + xb[1, here, :].astype(F32))
            mid[here, :] = middle
            n2[here, :] = (middle * lax.rsqrt(mean_square(middle) + EPS) * gain2[...]).astype(BF16)
            return carry

        for half in range(2):
            branch[half].wait_recv()
            in_rows(128, 32, lambda r, carry: norm_two(r + 128 * half, carry))
        for i in range(4):
            n2t[i] = n2[:, 256 * i:256 * i + 256].T
        gather("x")
        gather("y")
        for copy in loads[4:]:
            copy.wait()
        cot_here = cot[...].reshape(256, 1024)
        for t in range(0, 2304, TILE):
            cut = slice(t, t + TILE)
            pre_g[...] = jnp.dot(n2[...], wg[:, cut], preferred_element_type=F32)
            pre_u[...] = jnp.dot(n2[...], wu[:, cut], preferred_element_type=F32)
            grad_h[...] = lax.dot_general(cot_here, wd[cut, :], NT, preferred_element_type=F32)

            def act_rows(r, carry):
                here = pl.ds(r, 32)
                gate, up, grad = pre_g[here, :], pre_u[here, :], grad_h[here, :]
                sig = jax.nn.sigmoid(gate)
                act = gate * sig
                hid_s[here, :] = (act * up).astype(BF16)
                gg_s[here, :] = (grad * up * (sig * (1.0 + gate * (1.0 - sig)))).astype(BF16)
                ug_s[here, :] = (grad * act).astype(BF16)
                return carry

            in_rows(256, 32, act_rows)
            hidt[cut, :] = hid_s[...].T
            gatet[cut, :] = gg_s[...].T
            upt[cut, :] = ug_s[...].T
            ffn = jnp.dot(hid_s[...], wd[cut, :], preferred_element_type=F32)
            back = lax.dot_general(gg_s[...], wg[:, cut], NT, preferred_element_type=F32)
            back += lax.dot_general(ug_s[...], wu[:, cut], NT, preferred_element_type=F32)
            last = t + TILE == 2304
            if t > 0:
                ffn += ffn_acc[...]
                back += n2g_acc[...]
            if last:
                xn[0] = back.astype(BF16)
                xf[0] = ffn.astype(BF16)
            else:
                ffn_acc[...] = ffn
                n2g_acc[...] = back
        links.close()

    v = lambda *shape: pltpu.VMEM(shape, BF16)
    f = lambda *shape: pltpu.VMEM(shape, F32)
    pl.run_scoped(
        forward, v(1024, 2304), v(1024, 2304), v(2304, 1024),
        f(256, TILE), f(256, TILE), f(256, TILE), v(256, TILE), v(256, TILE), v(256, TILE),
        f(256, 1024), f(256, 1024),
    )

    def backward(g1, g2, u1, u2, d1, dt, d2, ia, ib, ic, oa, ob, oc):
        back_link = links.send(xn.at[0], xn.at[1], place.sibling())
        trade("z", hidt, hz)
        trade("x", gatet, gx)
        trade("y", upt, uy)
        ffn_link = links.send(xf.at[0], xf.at[1], place.sibling())
        share("z", cotz)
        back_link.wait_recv()
        ffn_link.wait_recv()
        small[...] = jnp.zeros((8, 1024), F32)

        def norm_two_back(i, total):
            here = pl.ds(pl.multiple_of(i * 32, 32), 32)
            grad = xn[0, here, :].astype(F32) + xn[1, here, :].astype(F32)
            middle = mid[here, :]
            ffn = xf[0, here, :].astype(F32) + xf[1, here, :].astype(F32)
            block_out[here, :] = (middle + ffn).astype(BF16)
            scale = lax.rsqrt(mean_square(middle) + EPS)
            unit = middle * scale
            total += jnp.sum((grad * unit).reshape(4, 8, 1024), axis=0)
            inner = grad * gain2[...]
            inner = scale * (inner - unit * jnp.mean(inner * unit, axis=-1, keepdims=True))
            middle = cot[i].astype(F32) + inner
            mid[here, :] = middle
            mlow[here, :] = middle.astype(BF16)
            return total

        total = lax.fori_loop(0, 8, norm_two_back, jnp.zeros((8, 1024), F32))
        small[1:2, :] = jnp.sum(total, axis=0, keepdims=True)
        mxg[...] = lax.dot_general(mlow[...], wout[...], NT, preferred_element_type=F32)

        def conv_back(r, totals):
            here = pl.ds(r, 32)
            grad = mxg[here, :]
            back = grad * proj[1, here, :]
            cgbuf[here, :] = back
            pg[here, 512:1024] = (grad * cv[here, :]).astype(BF16)
            return tuple(
                t + jnp.sum((back * g).reshape(4, 8, 512), axis=0) for t, g in zip(totals, shifted_gated(r))
            )

        totals = in_rows(256, 32, conv_back, (jnp.zeros((8, 512), F32),) * 3)
        edge = links.send(cgbuf.at[pl.ds(0, 8)], cgbuf.at[pl.ds(256, 8)], place.along[-1])
        for k in range(3):
            small[2 + k:3 + k, 0:512] = jnp.sum(totals[k], axis=0, keepdims=True)

        def out_tile(i, carry):
            res = jnp.dot(mixedt[i], mlow[...], preferred_element_type=F32)
            oa[i] = res.astype(BF16).reshape(8, 16, 1024)
            return carry

        lax.fori_loop(0, 4, out_tile, 0)
        out_ring = Ring(place, links, "z", halves_of(oa, 0, 1), oa1, oa2)
        out_ring.start()
        edge.wait_recv()
        cgbuf[pl.ds(256, 8), :] = cgbuf[pl.ds(256, 8), :] * carried_on

        def taps_back(r, carry):
            here = pl.ds(r, 32)
            window = cgbuf[pl.ds(r, 40), :]
            grad = (
                taps[2:3] * window[:32]
                + taps[1:2] * pltpu.roll(window, 39, 0)[:32]
                + taps[0:1] * pltpu.roll(window, 38, 0)[:32]
            )
            pg[here, 0:512] = (grad * proj[2, here, :]).astype(BF16)
            pg[here, 1024:1536] = (grad * proj[0, here, :]).astype(BF16)
            return carry

        in_rows(256, 32, taps_back)
        part = lax.dot_general(pg[:, 0:512], win[0], NT, preferred_element_type=F32)
        part += lax.dot_general(pg[:, 512:1024], win[1], NT, preferred_element_type=F32)
        part += lax.dot_general(pg[:, 1024:1536], win[2], NT, preferred_element_type=F32)
        xh[0] = part.astype(BF16)
        first_link = links.send(xh.at[0], xh.at[1], place.sibling())

        in_rings = [
            Ring(place, links, "z", lambda b, h: ia.at[0, b, pl.ds(2 * h, 2)], ia1.at[0], ia2.at[0]),
            Ring(place, links, "x", lambda b, h: ia.at[1, pl.ds(2 * h, 2), b], ia1.at[1], ia2.at[1]),
            Ring(place, links, "y", lambda b, h: ia.at[2, pl.ds(2 * h, 2), :, b], ia1.at[2], ia2.at[2]),
        ]
        for part in range(3):
            def in_tile(i, carry, part=part):
                res = jnp.dot(n1t[i], pg[:, part * 512:(part + 1) * 512], preferred_element_type=F32)
                ia[part, i] = res.astype(BF16).reshape(4, 4, 16, 512)
                return carry

            lax.fori_loop(0, 4, in_tile, 0)
            in_rings[part].start()

        def ready(axis):
            for shift in (1, 3, 2):
                shared[axis, shift].wait_recv()
                traded[axis, shift].wait_recv()

        share("x", n2x)
        share("y", n2y)
        first_link.wait_recv()

        def norm_one_back(r, total):
            here = pl.ds(r, 32)
            grad = xh[0, here, :].astype(F32) + xh[1, here, :].astype(F32)
            x = hin[here, :].astype(F32)
            scale = lax.rsqrt(mean_square(x) + EPS)
            unit = x * scale
            total += jnp.sum((grad * unit).reshape(4, 8, 1024), axis=0)
            inner = grad * gain1[...]
            inner = scale * (inner - unit * jnp.mean(inner * unit, axis=-1, keepdims=True))
            input_grad[here, :] = (mid[here, :] + inner).astype(BF16)
            return total

        total = in_rows(256, 32, norm_one_back, jnp.zeros((8, 1024), F32))
        small[0:1, :] = jnp.sum(total, axis=0, keepdims=True)
        small_links = [links.send(small, sm1.at[0, shift - 1], place.peer("z", shift)) for shift in (1, 3, 2)]

        def wide(own_x, got_x, own_g, got_g, me, store):
            def tile(i, carry):
                own = own_g[pl.ds(pl.multiple_of(me * 576, 576), 576), :]
                res = lax.dot_general(own_x[i], own, NT, preferred_element_type=F32)
                for d in range(3):
                    res += lax.dot_general(got_x[d, i], got_g[d], NT, preferred_element_type=F32)
                store(i, res.astype(BF16))
                return carry

            lax.fori_loop(0, 4, tile, 0)

        ready("z")

        def down_tile(i, carry):
            own = hidt[pl.ds(pl.multiple_of(place.coord["z"] * 576 + i * 144, 144), 144), :]
            res = jnp.dot(own, cot[...].reshape(256, 1024), preferred_element_type=F32)
            for d in range(3):
                got = hz[d, pl.ds(pl.multiple_of(i * 144, 144), 144), :]
                res += jnp.dot(got, cotz[d].reshape(256, 1024), preferred_element_type=F32)
            d1[i] = res.astype(BF16).reshape(9, 16, 1024)
            return carry

        lax.fori_loop(0, 4, down_tile, 0)
        down_ring = Ring(place, links, "x", halves_of(d1, 0, 3), d1a, d1b)
        down_ring.start()

        ready("x")

        def gate_store(i, res):
            g1[pl.ds(4 * i, 4)] = res.reshape(4, 4, 16, 576)

        wide(n2t, n2x, gatet, gx, place.coord["x"], gate_store)
        gate_ring = Ring(place, links, "y", halves_of(g1, 1, 0), g1a, g1b)
        gate_ring.start()

        ready("y")

        def up_store(i, res):
            u1[i] = res.reshape(16, 16, 576)

        wide(n2t, n2y, upt, uy, place.coord["y"], up_store)
        up_ring = Ring(place, links, "z", halves_of(u1, 0, 1), u1a, u1b)
        up_ring.start()

        for ring in in_rings:
            ring.pass_on()
        out_ring.pass_on()

        for copy in small_links:
            copy.wait_recv()
        sm2[0] = small[...] + sm1[0, 0] + sm1[0, 1] + sm1[0, 2]
        small_links = [links.send(sm2.at[0], sm1.at[1, shift - 1], place.peer("x", shift)) for shift in (1, 3, 2)]

        for half in range(2):
            ib[0, pl.ds(2 * half, 2)] = in_rings[0].total(half).astype(BF16)
        for half in range(2):
            ib[1, pl.ds(2 * half, 2)] = in_rings[1].total(half).astype(BF16)
        for half in range(2):
            ib[2, pl.ds(2 * half, 2)] = in_rings[2].total(half).astype(BF16)
        in_rings = [
            Ring(place, links, "x", halves_of(ib.at[0], 0, 1), ib1.at[0], ib2.at[0]),
            Ring(place, links, "y", halves_of(ib.at[1], 1, 0), ib1.at[1], ib2.at[1]),
            Ring(place, links, "z", halves_of(ib.at[2], 0, 1), ib1.at[2], ib2.at[2]),
        ]
        for ring in in_rings:
            ring.start()
        for half in range(2):
            ob[pl.ds(2 * half, 2)] = out_ring.total(half).astype(BF16).reshape(2, 2, 16, 1024)
        out_ring = Ring(place, links, "x", halves_of(ob, 0, 1), ob1, ob2)
        out_ring.start()

        down_ring.pass_on()
        gate_ring.pass_on()
        up_ring.pass_on()
        for ring in in_rings:
            ring.pass_on()
        out_ring.pass_on()

        for copy in small_links:
            copy.wait_recv()
        sm2[1] = sm2[0] + sm1[1, 0] + sm1[1, 1] + sm1[1, 2]
        small_links = [links.send(sm2.at[1], sm1.at[2, shift - 1], place.peer("y", shift)) for shift in (1, 3, 2)]

        dt[pl.ds(144, 16), :] = jnp.zeros((16, 1024), F32)
        for half in range(2):
            dt[pl.ds(0, 144), half * 512:(half + 1) * 512] = down_ring.total(half).reshape(144, 512)
        for y in range(4):
            d2[y] = dt[pl.ds(36 * y, 48), :].astype(BF16)
        down_ring = Ring(place, links, "y", halves_of(d2, 0, 2), d2a, d2b)
        down_ring.start()
        for half in range(2):
            g2[pl.ds(2 * half, 2)] = gate_ring.total(half).astype(BF16).reshape(2, 4, 16, 576)
        gate_ring = Ring(place, links, "z", halves_of(g2, 0, 1), g2a, g2b)
        gate_ring.start()
        for half in range(2):
            u2[pl.ds(2 * half, 2)] = up_ring.total(half).astype(BF16).reshape(2, 4, 16, 576)
        up_ring = Ring(place, links, "x", halves_of(u2, 0, 1), u2a, u2b)
        up_ring.start()
        for part in range(3):
            for half in range(2):
                ic[part, pl.ds(2 * half, 2)] = in_rings[part].total(half).astype(BF16)
        in_rings = [
            Ring(place, links, axis, halves_of(ic.at[part], 0, 2), ic1.at[part], ic2.at[part])
            for part, axis in enumerate("yzx")
        ]
        for ring in in_rings:
            ring.start()
        for half in range(2):
            res = out_ring.total(half).reshape(16, 1024).astype(BF16)
            for y in range(2):
                oc[2 * half + y] = jnp.concatenate([res[8 * y:8 * y + 8]] * 2, axis=0)
        out_ring = Ring(place, links, "y", halves_of(oc, 0, 2), oc1, oc2)
        out_ring.start()

        gate_ring.pass_on()
        up_ring.pass_on()
        down_ring.pass_on()
        for ring in in_rings:
            ring.pass_on()
        out_ring.pass_on()

        trades = []
        for ring, axis, own in ((gate_ring, "x", ga), (up_ring, "y", ua)):
            for half in range(2):
                own[0, pl.ds(2 * half, 2)] = ring.total(half)
            for shift in (1, 3, 2):
                block = place.blocks[axis][shift]
                trades.append(
                    links.send(own.at[0, block], own.at[1, place.coord[axis]], place.peer(axis, shift))
                )
        for half in range(2):
            down_out[:, half * 512:(half + 1) * 512] = down_ring.total(half)[:36]
        for part in range(3):
            for half in range(2):
                in_out[:, part, half * 256:(half + 1) * 256] = in_rings[part].total(half)
        for half in range(2):
            out_out[:, half * 512:(half + 1) * 512] = out_ring.total(half)[:8]
        for copy in small_links:
            copy.wait_recv()
        small_out[...] = sm2[1] + sm1[2, 0] + sm1[2, 1] + sm1[2, 2]
        for copy in trades:
            copy.wait_recv()
        for own, axis, out in ((ga, "x", gate_out), (ua, "y", up_out)):
            me = place.coord[axis]
            own[1, me] = own[0, me]
            out[...] = jnp.concatenate([own[1, p] for p in range(4)], axis=1)
        links.close()
        for copy in gathered.values():
            copy.wait_send()

    pl.run_scoped(
        backward,
        v(16, 4, 16, 576), v(4, 4, 16, 576), v(4, 16, 16, 576), v(4, 4, 16, 576),
        v(4, 9, 16, 1024), f(160, 1024), v(4, 48, 1024),
        v(3, 4, 4, 4, 16, 512), v(3, 4, 4, 16, 512), v(3, 4, 16, 512),
        v(4, 8, 16, 1024), v(4, 2, 16, 1024), v(4, 16, 1024),
    )


def finish_kernel(
    block_in, grad_in, gate_in, up_in, down_in, in_in, out_in, small_in,
    block_out, input_grad, gate_out, up_out, down_out, in_out, out_out, gain1_out, gain2_out, conv_out,
):
    place = lax.axis_index("seq")
    for src, dst in (
        (block_in, block_out), (grad_in, input_grad), (gate_in, gate_out), (up_in, up_out),
        (down_in, down_out), (in_in, in_out), (out_in, out_out),
    ):
        dst[...] = src[...]
    gains = pltpu.roll(small_in[...], 1024 - 16 * place, 1)
    gain1_out[...] = gains[0:1, 0:16]
    gain2_out[...] = gains[1:2, 0:16]
    taps = pltpu.roll(small_in[...], 1024 - 8 * place, 1)
    conv_out[...] = taps[:, 0:128].T[0:8, 2:5]


def shards(
    hidden_in, norm1_gain, in_weight, conv_weight, out_weight, norm2_gain, gate_weight, up_weight, down_weight,
    cotangent,
):
    v = lambda *shape: pltpu.VMEM(shape, BF16)
    f = lambda *shape: pltpu.VMEM(shape, F32)

    def ring(*half):
        return [v(2, *half), v(2, 2, *half)]

    scratch = [
        v(3, 1024, 512), v(512, 1024), v(256, 1024), v(4, 256, 256), v(256, 1024), v(4, 256, 256),
        v(2304, 256), v(2304, 256), v(2304, 256), f(3, 256, 512), v(272, 512), f(256, 512), v(256, 512),
        v(4, 128, 256), f(256, 1024), v(256, 1024), f(264, 512), f(256, 512), v(256, 1536), f(8, 1024),
        *[v(2, 256, 1024)] * 4,
        v(3, 4, 256, 256), v(3, 4, 256, 256), v(3, 8, 32, 1024),
        v(3, 576, 256), v(3, 576, 256), v(3, 576, 256),
        *ring(8, 16, 576), *ring(2, 16, 576), f(2, 4, 16, 576),
        *ring(8, 16, 576), *ring(2, 16, 576), f(2, 4, 16, 576),
        *ring(9, 16, 512), *ring(48, 512),
        v(3, 2, 2, 4, 16, 512), v(3, 2, 2, 2, 4, 16, 512),
        v(3, 2, 2, 16, 512), v(3, 2, 2, 2, 16, 512),
        v(3, 2, 16, 256), v(3, 2, 2, 16, 256),
        *ring(4, 16, 1024), *ring(1, 16, 1024), *ring(16, 512),
        f(3, 3, 8, 1024), f(2, 8, 1024),
        pltpu.SemaphoreType.DMA((N_SEMS,)), pltpu.SemaphoreType.DMA((N_SEMS,)), pltpu.SemaphoreType.DMA((7,)),
    ]
    vmem = pl.BlockSpec(memory_space=pltpu.VMEM)
    far = pl.BlockSpec(memory_space=pl.ANY)
    (
        block_out, input_grad, gate_final, up_final, down_final, in_final, out_final, small_final,
    ) = pl.pallas_call(
        block_kernel,
        out_shape=[jax.ShapeDtypeStruct((256, 1024), BF16)] * 2
        + [
            jax.ShapeDtypeStruct(shape, F32)
            for shape in ((16, 2304), (16, 2304), (36, 1024), (16, 3, 512), (8, 1024), (8, 1024))
        ],
        in_specs=[vmem, vmem, far, vmem, far, vmem, far, far, far, vmem],
        out_specs=[vmem] * 8,
        scratch_shapes=scratch,
        compiler_params=pltpu.CompilerParams(
            collective_id=0, has_side_effects=True, vmem_limit_bytes=62 * 2**20
        ),
        name="block",
    )(
        hidden_in, norm1_gain.reshape(1, 1024), in_weight.transpose(1, 0, 2), conv_weight.T, out_weight,
        norm2_gain.reshape(1, 1024), gate_weight, up_weight, down_weight, cotangent.reshape(8, 32, 1024),
    )
    (
        block_out, input_grad, gate_final, up_final, down_final, in_final, out_final, gain1_final, gain2_final,
        conv_final,
    ) = pl.pallas_call(
        finish_kernel,
        out_shape=[jax.ShapeDtypeStruct((256, 1024), BF16)] * 2
        + [
            jax.ShapeDtypeStruct(shape, F32)
            for shape in (
                (16, 2304), (16, 2304), (36, 1024), (16, 3, 512), (8, 1024), (1, 16), (1, 16), (8, 3),
            )
        ],
        in_specs=[vmem] * 8,
        out_specs=[vmem] * 10,
        name="finish",
    )(block_out, input_grad, gate_final, up_final, down_final, in_final, out_final, small_final)
    return (
        block_out,
        input_grad,
        gain1_final.reshape(16),
        in_final,
        conv_final,
        out_final,
        gain2_final.reshape(16),
        gate_final,
        up_final,
        down_final,
    )


def solution(mesh):
    placed = (
        P("seq", None),
        P(),
        P(None, None, "head"),
        P("head", None),
        P("head", None),
        P(),
        P(None, "head"),
        P(None, "head"),
        P("head", None),
        P("seq", None),
    )
    return jax.shard_map(
        shards,
        mesh=mesh,
        in_specs=placed,
        out_specs=(
            P("seq", None),
            P("seq", None),
            P("seq"),
            P("seq", None, "head"),
            P(("head", "seq"), None),
            P(("head", "seq"), None),
            P("seq"),
            P("seq", "head"),
            P("seq", "head"),
            P(("head", "seq"), None),
        ),
        check_vma=False,
    )
```

time: 1180 us -> 103 us (0.09)
  blocking collectives: 584 us -> 0 us
  waiting for transfers between devices: 465 us -> 0 us
  Pallas kernels: 0 us -> 99.5 us
  matrix products: 49.5 us -> 0 us
  local copies, waits for them, and re-layouts: 35.2 us -> 2.92 us
  between operations: 16.7 us -> 0.66 us
  starting transfers between devices: 15.2 us -> 0 us
  other arithmetic: 13.3 us -> 0 us
    unnamed x2 -> x0, blocking collectives: 584 us -> none
    reduce_scatter x3 -> x0, waiting for transfers between devices: 409 us -> none  [the longest x1 230 us: shards(): lax.psum_scatter(gate_w_grad, 'seq', scatter_dimension=0, tiled=True)]
    pallas_call x0 -> x2, Pallas kernels: none -> 99.5 us  [the longest x1 96.8 us: shards(): pl.pallas_call(block_kernel, out_shape=[jax.ShapeDtypeStruct((256, 1024),...]
    psum x3 -> x0, waiting for transfers between devices: 54.1 us -> none  [the longest x1 28.3 us: shards(): lax.psum(jnp.dot(mixed, out_weight, preferred_element_type=f32), 'head')]
    dot_general x15 -> x0, matrix products: 49.5 us -> none  [the longest x1 6.39 us: shards(): jnp.einsum('td,tf->df', normed_two, up_grad, preferred_element_type=f32)]
    unnamed x70 -> x2, local copies, waits for them, and re-layouts: 25.8 us -> 2.92 us
  transfers between devices with their start and end apart: 16 -> 0, of which waited for: 6 -> 0; matrix products, arithmetic and copies ran while one was open for 25% -> 0% of each run, Pallas kernels for 0% -> 0%
where the time goes in v2:
time: 103 us
  Pallas kernels  99.5 us (97%)
  local copies, waits for them, and re-layouts  2.92 us (3%)
    pallas_call x1, Pallas kernels, shards(): pl.pallas_call(block_kernel, out_shape=[jax.ShapeDtypeStruct((256, 1024),...  96.8 us
    unnamed x2, local copies, waits for them, and re-layouts  2.92 us
    pallas_call x1, Pallas kernels, shards(): pl.pallas_call(finish_kernel, out_shape=[jax.ShapeDtypeStruct((256, 1024)...  2.75 us

profile of v2, /device:TPU:0, one launch (start us, length us, event | category | flops | bytes accessed | tf_op | source)
XLA Modules:
  0.0 103.1 jit_solution(4781728164404599442)
XLA Ops:
  0.6 96.8 %block.1 = (bf16[256,1024]{1,0:T(8,128)(2,1)}, bf16[256,1024]{1,0:T(8,128)(2,1)}, f32[16,2304]{1,0:T(8,128)}, f32[16,2304]{1,0:T(8,128)}, f32[36,1024]{1,0:T(8,1...) custom-call(bf16[256,1024]{1,0:T(8,128)(2,1)} %hin.1, f32[1,1024]{1,0:T(1,128)} %bitcast.10, ...), custom_call_target="tpu_custom_call" | custom-call | tf_op jit(solution)/shard_map/block/pallas_call | solution.py:632
  97.4 2.7 %finish.1 = (bf16[256,1024]{1,0:T(8,128)(2,1)}, bf16[256,1024]{1,0:T(8,128)(2,1)}, f32[16,2304]{1,0:T(8,128)}, f32[16,2304]{1,0:T(8,128)}, f32[36,1024]{1,0:T(8,...) custom-call(bf16[256,1024]{1,0:T(8,128)(2,1)} %get-tuple-element.28., ...), custom_call_target="tpu_custom_call" | custom-call | tf_op jit(solution)/shard_map/finish/pallas_call | solution.py:653
  100.2 1.3 %copy.21 = f32[8,3]{0,1:T(4,128)} copy(f32[8,3]{1,0:T(8,128)} %get-tuple-element.50) | data formatting | bytes 192
  101.5 1.6 %copy.20 = f32[16,3,512]{2,0,1:T(8,128)} copy(f32[16,3,512]{2,1,0:T(4,128)} %get-tuple-element.49) | data formatting | bytes 196608

commit v3 on v2

--- a/solution.py
+++ b/solution.py
@@ -10,8 +10,9 @@
 F32 = jnp.float32
 BF16 = jnp.bfloat16
 NT = (((1,), (1,)), ((), ()))
-N_SEMS = 180
+N_SEMS = 210
 TILE = 768
+CUTS = (0, 256, 896, 1536)
 
 
 class Place:
@@ -41,6 +42,12 @@
     def peer(self, axis, shift):
         return self.peers[axis, shift]
 
+    def diagonal(self, first, shift, second, other):
+        moved = dict(self.coord)
+        moved[first] = self.blocks[first][shift]
+        moved[second] = self.blocks[second][other]
+        return ((moved["z"] * 4 + moved["x"]) * 4 + moved["y"], self.head)
+
     def sibling(self):
         return (self.seq, 1 - self.head)
 
@@ -113,6 +120,24 @@
         return own + self.second[0, half].astype(F32) + self.second[1, half].astype(F32)
 
 
+class Plane:
+    def __init__(self, place, links, axes, src, got):
+        first, second = axes
+        here = (place.coord[first], place.coord[second])
+        self.copies = []
+        for shift in (2, 1, 3, 0):
+            for other in (2, 1, 3, 0):
+                if shift or other:
+                    there = src.at[place.blocks[first][shift], place.blocks[second][other]]
+                    device = place.diagonal(first, shift, second, other)
+                    self.copies.append(links.send(there, got.at[here[0], here[1]], device))
+        got[here[0], here[1]] = src[here[0], here[1]]
+
+    def wait(self):
+        for copy in self.copies:
+            copy.wait_recv()
+
+
 def halves_of(ref, axis_dim, half_dim):
     extent = ref.shape[half_dim] // 2
 
@@ -142,11 +167,8 @@
     win, wout, n1, n1t, n2, n2t, hidt, gatet, upt, proj, gbuf, cv, mixed, mixedt, mid, mlow, cgbuf, mxg, pg,
     small, xb, xf, xn, xh,
     n2x, n2y, cotz, gx, uy, hz,
-    g1a, g1b, g2a, g2b, ga,
-    u1a, u1b, u2a, u2b, ua,
-    d1a, d1b, d2a, d2b,
-    ia1, ia2, ib1, ib2, ic1, ic2,
-    oa1, oa2, ob1, ob2, oc1, oc2,
+    g1a, g1b, g3, u1a, u1b, u3, d1a, d1b, d3,
+    ia1, ia2, ib1, ib2, i3, ja1, ja2, jb1, jb2, j3, ka1, ka2, kb1, kb2, k3, oa1, oa2, ob1, ob2, o3,
     sm1, sm2,
     send_sem, recv_sem, load_sem,
 ):
@@ -155,6 +177,8 @@
     head = place.head
     barrier = pltpu.get_barrier_semaphore()
     peers = [place.peer(axis, shift) for axis in "zxy" for shift in (1, 2, 3)]
+    for first, second in ("zx", "xy"):
+        peers += [place.diagonal(first, i, second, j) for i in (1, 2, 3) for j in (1, 2, 3)]
     peers += [place.sibling(), place.along[1], place.along[-1]]
     carried = jnp.where(lax.rem(place.seq, 16) != 0, 1.0, 0.0).astype(F32)
     carried_on = jnp.where(lax.rem(place.seq, 16) != 15, 1.0, 0.0).astype(F32)
@@ -165,14 +189,24 @@
     for axis, src, dst in (("z", cot, cotz), ("x", n2t, n2x), ("y", n2t, n2y)):
         part = src.shape[0] // 2
         mine = pl.ds(part * head, part)
-        for shift in (1, 3, 2):
+        for shift in (1, 3, 2) if axis == "z" else (1, 3):
             gathered[axis, shift] = links.plan(
                 src.at[mine], dst.at[shift - 1, mine], place.peer(axis, shift)
             )
+        if axis != "z":
+            for shift, here in ((1, 2 * head), (3, 2 * head + 1)):
+                gathered[axis, 2, shift] = links.plan(
+                    dst.at[shift - 1, here], dst.at[1, here], place.peer(axis, shift)
+                )
 
     def gather(axis):
-        for shift in (1, 3, 2):
+        for shift in (1, 3, 2) if axis == "z" else (1, 3):
             gathered[axis, shift].start()
+
+    def relay(axis):
+        for shift in (1, 3):
+            gathered[axis, shift].wait_recv()
+            gathered[axis, 2, shift].start()
 
     def trade(axis, src, dst):
         for shift in (1, 3, 2):
@@ -182,7 +216,11 @@
 
     def share(axis, dst):
         for shift in (1, 3, 2):
-            gathered[axis, shift].wait_recv()
+            if axis == "z":
+                gathered[axis, shift].wait_recv()
+            elif shift == 2:
+                gathered[axis, 2, 1].wait_recv()
+                gathered[axis, 2, 3].wait_recv()
             part = dst.shape[1] // 2
             here = dst.at[shift - 1, pl.ds(part * head, part)]
             shared[axis, shift] = links.send(here, here, place.sibling())
@@ -199,9 +237,9 @@
             (w_in.at[0], win.at[0]), (w_in.at[1], win.at[1]), (w_in.at[2], win.at[2]),
             (w_out, wout), (w_gate, wg), (w_up, wu), (w_down, wd),
         ):
-            copy = pltpu.make_async_copy(src, dst, load_sem.at[len(loads)])
+            loads.append(pltpu.make_async_copy(src, dst, load_sem.at[len(loads)]))
+        for copy in loads[:4]:
             copy.start()
-            loads.append(copy)
         for device in peers:
             pl.semaphore_signal(barrier, inc=1, device_id=device, device_id_type=MESH)
 
@@ -215,6 +253,9 @@
         gather("z")
         for part in (0, 2, 1):
             loads[part].wait()
+            if part == 2:
+                for copy in loads[4:]:
+                    copy.start()
             proj[part] = jnp.dot(n1[...], win[part], preferred_element_type=F32)
             if part == 2:
                 def gate_rows(r, carry):
@@ -269,6 +310,9 @@
             pre_g[...] = jnp.dot(n2[...], wg[:, cut], preferred_element_type=F32)
             pre_u[...] = jnp.dot(n2[...], wu[:, cut], preferred_element_type=F32)
             grad_h[...] = lax.dot_general(cot_here, wd[cut, :], NT, preferred_element_type=F32)
+            if t + TILE == 2304:
+                relay("x")
+                relay("y")
 
             def act_rows(r, carry):
                 here = pl.ds(r, 32)
@@ -307,7 +351,7 @@
         f(256, 1024), f(256, 1024),
     )
 
-    def backward(g1, g2, u1, u2, d1, dt, d2, ia, ib, ic, oa, ob, oc):
+    def backward(g1, g2, u1, u2, d1, dt, d2, ia, ib, ic, ja, jb, jc, ka, kb, kc, oa, ob, oc):
         back_link = links.send(xn.at[0], xn.at[1], place.sibling())
         trade("z", hidt, hz)
         trade("x", gatet, gx)
@@ -384,14 +428,14 @@
         first_link = links.send(xh.at[0], xh.at[1], place.sibling())
 
         in_rings = [
-            Ring(place, links, "z", lambda b, h: ia.at[0, b, pl.ds(2 * h, 2)], ia1.at[0], ia2.at[0]),
-            Ring(place, links, "x", lambda b, h: ia.at[1, pl.ds(2 * h, 2), b], ia1.at[1], ia2.at[1]),
-            Ring(place, links, "y", lambda b, h: ia.at[2, pl.ds(2 * h, 2), :, b], ia1.at[2], ia2.at[2]),
+            Ring(place, links, "z", lambda b, h: ia.at[b, pl.ds(2 * h, 2)], ia1, ia2),
+            Ring(place, links, "x", lambda b, h: ja.at[pl.ds(2 * h, 2), b], ja1, ja2),
+            Ring(place, links, "y", lambda b, h: ka.at[pl.ds(2 * h, 2), :, b], ka1, ka2),
         ]
-        for part in range(3):
-            def in_tile(i, carry, part=part):
-                res = jnp.dot(n1t[i], pg[:, part * 512:(part + 1) * 512], preferred_element_type=F32)
-                ia[part, i] = res.astype(BF16).reshape(4, 4, 16, 512)
+        for part, own in enumerate((ia, ja, ka)):
+            def in_tile(i, carry, own=own, left=CUTS[part], right=CUTS[part + 1]):
+                res = jnp.dot(n1t[i], pg[:, left:right], preferred_element_type=F32)
+                own[i] = res.astype(BF16).reshape(4, 4, 16, right - left)
                 return carry
 
             lax.fori_loop(0, 4, in_tile, 0)
@@ -448,6 +492,10 @@
         down_ring = Ring(place, links, "x", halves_of(d1, 0, 3), d1a, d1b)
         down_ring.start()
 
+        for ring in in_rings:
+            ring.pass_on()
+        out_ring.pass_on()
+
         ready("x")
 
         def gate_store(i, res):
@@ -465,41 +513,30 @@
         wide(n2t, n2y, upt, uy, place.coord["y"], up_store)
         up_ring = Ring(place, links, "z", halves_of(u1, 0, 1), u1a, u1b)
         up_ring.start()
-
-        for ring in in_rings:
-            ring.pass_on()
-        out_ring.pass_on()
 
         for copy in small_links:
             copy.wait_recv()
         sm2[0] = small[...] + sm1[0, 0] + sm1[0, 1] + sm1[0, 2]
         small_links = [links.send(sm2.at[0], sm1.at[1, shift - 1], place.peer("x", shift)) for shift in (1, 3, 2)]
-
+        down_ring.pass_on()
+
+        gate_ring.pass_on()
+        up_ring.pass_on()
+        for ring, own in zip(in_rings, (ib, jb, kb)):
+            for half in range(2):
+                own[pl.ds(2 * half, 2)] = ring.total(half).astype(BF16)
         for half in range(2):
-            ib[0, pl.ds(2 * half, 2)] = in_rings[0].total(half).astype(BF16)
-        for half in range(2):
-            ib[1, pl.ds(2 * half, 2)] = in_rings[1].total(half).astype(BF16)
-        for half in range(2):
-            ib[2, pl.ds(2 * half, 2)] = in_rings[2].total(half).astype(BF16)
+            res = out_ring.total(half).reshape(2, 4, 8, 1024)
+            res = jnp.concatenate([res[..., :512], res[..., 512:]], axis=2)
+            ob[pl.ds(2 * half, 2)] = res.astype(BF16)
         in_rings = [
-            Ring(place, links, "x", halves_of(ib.at[0], 0, 1), ib1.at[0], ib2.at[0]),
-            Ring(place, links, "y", halves_of(ib.at[1], 1, 0), ib1.at[1], ib2.at[1]),
-            Ring(place, links, "z", halves_of(ib.at[2], 0, 1), ib1.at[2], ib2.at[2]),
+            Ring(place, links, "x", halves_of(ib, 0, 1), ib1, ib2),
+            Ring(place, links, "y", halves_of(jb, 1, 0), jb1, jb2),
+            Ring(place, links, "z", halves_of(kb, 0, 1), kb1, kb2),
+            Ring(place, links, "x", halves_of(ob, 0, 1), ob1, ob2),
         ]
         for ring in in_rings:
             ring.start()
-        for half in range(2):
-            ob[pl.ds(2 * half, 2)] = out_ring.total(half).astype(BF16).reshape(2, 2, 16, 1024)
-        out_ring = Ring(place, links, "x", halves_of(ob, 0, 1), ob1, ob2)
-        out_ring.start()
-
-        down_ring.pass_on()
-        gate_ring.pass_on()
-        up_ring.pass_on()
-        for ring in in_rings:
-            ring.pass_on()
-        out_ring.pass_on()
-
         for copy in small_links:
             copy.wait_recv()
         sm2[1] = sm2[0] + sm1[1, 0] + sm1[1, 1] + sm1[1, 2]
@@ -510,64 +547,53 @@
             dt[pl.ds(0, 144), half * 512:(half + 1) * 512] = down_ring.total(half).reshape(144, 512)
         for y in range(4):
             d2[y] = dt[pl.ds(36 * y, 48), :].astype(BF16)
-        down_ring = Ring(place, links, "y", halves_of(d2, 0, 2), d2a, d2b)
-        down_ring.start()
+        down_links = [
+            links.send(d2.at[place.blocks["y"][shift]], d3.at[shift - 1], place.peer("y", shift))
+            for shift in (2, 1, 3)
+        ]
         for half in range(2):
             g2[pl.ds(2 * half, 2)] = gate_ring.total(half).astype(BF16).reshape(2, 4, 16, 576)
-        gate_ring = Ring(place, links, "z", halves_of(g2, 0, 1), g2a, g2b)
-        gate_ring.start()
+        gate_plane = Plane(place, links, "zx", g2, g3)
         for half in range(2):
             u2[pl.ds(2 * half, 2)] = up_ring.total(half).astype(BF16).reshape(2, 4, 16, 576)
-        up_ring = Ring(place, links, "x", halves_of(u2, 0, 1), u2a, u2b)
-        up_ring.start()
-        for part in range(3):
-            for half in range(2):
-                ic[part, pl.ds(2 * half, 2)] = in_rings[part].total(half).astype(BF16)
-        in_rings = [
-            Ring(place, links, axis, halves_of(ic.at[part], 0, 2), ic1.at[part], ic2.at[part])
-            for part, axis in enumerate("yzx")
-        ]
-        for ring in in_rings:
-            ring.start()
-        for half in range(2):
-            res = out_ring.total(half).reshape(16, 1024).astype(BF16)
-            for y in range(2):
-                oc[2 * half + y] = jnp.concatenate([res[8 * y:8 * y + 8]] * 2, axis=0)
-        out_ring = Ring(place, links, "y", halves_of(oc, 0, 2), oc1, oc2)
-        out_ring.start()
-
-        gate_ring.pass_on()
-        up_ring.pass_on()
-        down_ring.pass_on()
+        up_plane = Plane(place, links, "xy", u2, u3)
+
         for ring in in_rings:
             ring.pass_on()
-        out_ring.pass_on()
-
-        trades = []
-        for ring, axis, own in ((gate_ring, "x", ga), (up_ring, "y", ua)):
-            for half in range(2):
-                own[0, pl.ds(2 * half, 2)] = ring.total(half)
-            for shift in (1, 3, 2):
-                block = place.blocks[axis][shift]
-                trades.append(
-                    links.send(own.at[0, block], own.at[1, place.coord[axis]], place.peer(axis, shift))
-                )
-        for half in range(2):
-            down_out[:, half * 512:(half + 1) * 512] = down_ring.total(half)[:36]
-        for part in range(3):
-            for half in range(2):
-                in_out[:, part, half * 256:(half + 1) * 256] = in_rings[part].total(half)
-        for half in range(2):
-            out_out[:, half * 512:(half + 1) * 512] = out_ring.total(half)[:8]
         for copy in small_links:
             copy.wait_recv()
         small_out[...] = sm2[1] + sm1[2, 0] + sm1[2, 1] + sm1[2, 2]
-        for copy in trades:
+        in_links = []
+        lines = (("y", ic, i3), ("z", jc, j3), ("x", kc, k3), ("y", oc, o3))
+        for ring, (axis, own, got) in zip(in_rings, lines):
+            for half in range(2):
+                own[pl.ds(2 * half, 2)] = ring.total(half).astype(BF16)
+            for shift in (2, 1, 3):
+                there = own.at[place.blocks[axis][shift]]
+                in_links.append(links.send(there, got.at[shift - 1], place.peer(axis, shift)))
+        for copy in down_links:
             copy.wait_recv()
-        for own, axis, out in ((ga, "x", gate_out), (ua, "y", up_out)):
-            me = place.coord[axis]
-            own[1, me] = own[0, me]
-            out[...] = jnp.concatenate([own[1, p] for p in range(4)], axis=1)
+        res = d2[place.coord["y"]].astype(F32)
+        for d in range(3):
+            res += d3[d].astype(F32)
+        down_out[...] = res[:36]
+        gate_plane.wait()
+        gate_out[...] = jnp.concatenate([jnp.sum(g3[:, x].astype(F32), axis=0) for x in range(4)], axis=1)
+        up_plane.wait()
+        up_out[...] = jnp.concatenate([jnp.sum(u3[:, y].astype(F32), axis=0) for y in range(4)], axis=1)
+        for copy in in_links:
+            copy.wait_recv()
+        sums = []
+        for axis, own, got in lines:
+            res = own[place.coord[axis]].astype(F32)
+            for d in range(3):
+                res += got[d].astype(F32)
+            sums.append(res)
+        res = jnp.concatenate(sums[:3], axis=1)
+        for part in range(3):
+            in_out[part] = res[:, 512 * part:512 * part + 512]
+        out_out[:, 0:512] = sums[3][:8]
+        out_out[:, 512:1024] = sums[3][8:]
         links.close()
         for copy in gathered.values():
             copy.wait_send()
@@ -576,8 +602,8 @@
         backward,
         v(16, 4, 16, 576), v(4, 4, 16, 576), v(4, 16, 16, 576), v(4, 4, 16, 576),
         v(4, 9, 16, 1024), f(160, 1024), v(4, 48, 1024),
-        v(3, 4, 4, 4, 16, 512), v(3, 4, 4, 16, 512), v(3, 4, 16, 512),
-        v(4, 8, 16, 1024), v(4, 2, 16, 1024), v(4, 16, 1024),
+        *[v(*([4] * dims), 16, width) for width in (256, 640, 640) for dims in (3, 2, 1)],
+        v(4, 8, 16, 1024), v(4, 4, 16, 512), v(4, 16, 512),
     )
 
 
@@ -595,7 +621,7 @@
     gain1_out[...] = gains[0:1, 0:16]
     gain2_out[...] = gains[1:2, 0:16]
     taps = pltpu.roll(small_in[...], 1024 - 8 * place, 1)
-    conv_out[...] = taps[:, 0:128].T[0:8, 2:5]
+    conv_out[...] = taps[2:5, 0:8]
 
 
 def shards(
@@ -615,13 +641,13 @@
         *[v(2, 256, 1024)] * 4,
         v(3, 4, 256, 256), v(3, 4, 256, 256), v(3, 8, 32, 1024),
         v(3, 576, 256), v(3, 576, 256), v(3, 576, 256),
-        *ring(8, 16, 576), *ring(2, 16, 576), f(2, 4, 16, 576),
-        *ring(8, 16, 576), *ring(2, 16, 576), f(2, 4, 16, 576),
-        *ring(9, 16, 512), *ring(48, 512),
-        v(3, 2, 2, 4, 16, 512), v(3, 2, 2, 2, 4, 16, 512),
-        v(3, 2, 2, 16, 512), v(3, 2, 2, 2, 16, 512),
-        v(3, 2, 16, 256), v(3, 2, 2, 16, 256),
-        *ring(4, 16, 1024), *ring(1, 16, 1024), *ring(16, 512),
+        *ring(8, 16, 576), v(4, 4, 16, 576), *ring(8, 16, 576), v(4, 4, 16, 576), *ring(9, 16, 512), v(3, 48, 1024),
+        *[
+            buffer
+            for width in (256, 640, 640)
+            for buffer in (*ring(2, 4, 16, width), *ring(2, 16, width), v(3, 16, width))
+        ],
+        *ring(4, 16, 1024), *ring(2, 16, 512), v(3, 16, 512),
         f(3, 3, 8, 1024), f(2, 8, 1024),
         pltpu.SemaphoreType.DMA((N_SEMS,)), pltpu.SemaphoreType.DMA((N_SEMS,)), pltpu.SemaphoreType.DMA((7,)),
     ]
@@ -634,7 +660,7 @@
         out_shape=[jax.ShapeDtypeStruct((256, 1024), BF16)] * 2
         + [
             jax.ShapeDtypeStruct(shape, F32)
-            for shape in ((16, 2304), (16, 2304), (36, 1024), (16, 3, 512), (8, 1024), (8, 1024))
+            for shape in ((16, 2304), (16, 2304), (36, 1024), (3, 16, 512), (8, 1024), (8, 1024))
         ],
         in_specs=[vmem, vmem, far, vmem, far, vmem, far, far, far, vmem],
         out_specs=[vmem] * 8,
@@ -656,7 +682,7 @@
         + [
             jax.ShapeDtypeStruct(shape, F32)
             for shape in (
-                (16, 2304), (16, 2304), (36, 1024), (16, 3, 512), (8, 1024), (1, 16), (1, 16), (8, 3),
+                (16, 2304), (16, 2304), (36, 1024), (3, 16, 512), (8, 1024), (1, 16), (1, 16), (3, 8),
             )
         ],
         in_specs=[vmem] * 8,
@@ -667,8 +693,8 @@
         block_out,
         input_grad,
         gain1_final.reshape(16),
-        in_final,
-        conv_final,
+        in_final.transpose(1, 0, 2),
+        conv_final.T,
         out_final,
         gain2_final.reshape(16),
         gate_final,

time: 103 us -> 96.8 us (0.940)
  Pallas kernels: 99.5 us -> 95.8 us
  local copies, waits for them, and re-layouts: 2.92 us -> 0 us
    pallas_call x1, Pallas kernels: 96.8 us -> 93.2 us  [shards(): pl.pallas_call(block_kernel, out_shape=[jax.ShapeDtypeStruct((256, 1024),...]
    unnamed x2 -> x0, local copies, waits for them, and re-layouts: 2.92 us -> none
where the time goes in v3:
time: 96.8 us; the launch traced here: 96.6 us
  Pallas kernels  95.8 us (99%)
    pallas_call x1, Pallas kernels, shards(): pl.pallas_call(block_kernel, out_shape=[jax.ShapeDtypeStruct((256, 1024),...  93.2 us
    pallas_call x1, Pallas kernels, shards(): pl.pallas_call(finish_kernel, out_shape=[jax.ShapeDtypeStruct((256, 1024)...  2.64 us

profile of v3, /device:TPU:0, one launch (start us, length us, event | category | flops | bytes accessed | tf_op | source)
XLA Modules:
  0.0 96.6 jit_solution(605504151884116375)
XLA Ops:
  0.6 93.2 %block.1 = (bf16[256,1024]{1,0:T(8,128)(2,1)}, bf16[256,1024]{1,0:T(8,128)(2,1)}, f32[16,2304]{1,0:T(8,128)}, f32[16,2304]{1,0:T(8,128)}, f32[36,1024]{1,0:T(8,1...) custom-call(bf16[256,1024]{1,0:T(8,128)(2,1)} %hin.1, f32[1,1024]{1,0:T(1,128)} %bitcast.12, ...), custom_call_target="tpu_custom_call" | custom-call | tf_op jit(solution)/shard_map/block/pallas_call | solution.py:658
  93.8 2.6 %finish.1 = (bf16[256,1024]{1,0:T(8,128)(2,1)}, bf16[256,1024]{1,0:T(8,128)(2,1)}, f32[16,2304]{1,0:T(8,128)}, f32[16,2304]{1,0:T(8,128)}, f32[36,1024]{1,0:T(8,...) custom-call(bf16[256,1024]{1,0:T(8,128)(2,1)} %get-tuple-element.28., ...), custom_call_target="tpu_custom_call" | custom-call | tf_op jit(solution)/shard_map/finish/pallas_call | solution.py:679

commit v4 on v3

--- a/solution.py
+++ b/solution.py
@@ -208,11 +208,12 @@
             gathered[axis, shift].wait_recv()
             gathered[axis, 2, shift].start()
 
-    def trade(axis, src, dst):
+    for axis, src, dst in (("z", hidt, hz), ("x", gatet, gx), ("y", upt, uy)):
         for shift in (1, 3, 2):
-            block = place.blocks[axis][shift]
-            rows = pl.ds(pl.multiple_of(block * 576, 576), 576)
-            traded[axis, shift] = links.send(src.at[rows], dst.at[shift - 1], place.peer(axis, shift))
+            rows = pl.ds(pl.multiple_of(place.blocks[axis][shift] * 576, 576), 576)
+            traded[axis, shift] = links.plan(src.at[rows], dst.at[shift - 1], place.peer(axis, shift))
+    back_link = links.plan(xn.at[0], xn.at[1], place.sibling())
+    ffn_link = links.plan(xf.at[0], xf.at[1], place.sibling())
 
     def share(axis, dst):
         for shift in (1, 3, 2):
@@ -231,11 +232,11 @@
         window = gbuf[pl.ds(r, 48), :].astype(F32)
         return [pltpu.roll(window, 2, 0)[16:], pltpu.roll(window, 1, 0)[16:], window[16:]]
 
-    def forward(wg, wu, wd, pre_g, pre_u, grad_h, hid_s, gg_s, ug_s, ffn_acc, n2g_acc):
+    def forward(wg, wu, wd, pre_g, pre_u, grad_h, hid_s, gg_s, ug_s, n2g_acc):
         loads = []
         for src, dst in (
             (w_in.at[0], win.at[0]), (w_in.at[1], win.at[1]), (w_in.at[2], win.at[2]),
-            (w_out, wout), (w_gate, wg), (w_up, wu), (w_down, wd),
+            (w_out, wout), (w_down, wd), (w_gate, wg), (w_up, wu),
         ):
             loads.append(pltpu.make_async_copy(src, dst, load_sem.at[len(loads)]))
         for copy in loads[:4]:
@@ -268,6 +269,16 @@
         for i in range(4):
             n1t[i] = n1[:, 256 * i:256 * i + 256].T
         loads[3].wait()
+        loads[4].wait()
+
+        def hidden_grad(tile):
+            part = wd[tile * TILE:tile * TILE + TILE, :]
+            grad_h[tile] = lax.dot_general(
+                cot[...].reshape(256, 1024), part, NT, preferred_element_type=F32
+            )
+
+        hidden_grad(0)
+        hidden_grad(1)
         edge.wait_recv()
         gbuf[pl.ds(0, 16), :] = (gbuf[pl.ds(0, 16), :].astype(F32) * carried).astype(BF16)
 
@@ -288,6 +299,8 @@
         for i in range(4):
             mixedt[i] = mixed[:, 128 * i:128 * i + 128].T
 
+        hidden_grad(2)
+
         def norm_two(r, carry):
             here = pl.ds(r, 32)
             middle = hin[here, :].astype(F32) + (xb[0, here, :].astype(F32) + xb[1, here, :].astype(F32))
@@ -302,61 +315,56 @@
             n2t[i] = n2[:, 256 * i:256 * i + 256].T
         gather("x")
         gather("y")
-        for copy in loads[4:]:
+        for copy in loads[5:]:
             copy.wait()
-        cot_here = cot[...].reshape(256, 1024)
         for t in range(0, 2304, TILE):
             cut = slice(t, t + TILE)
             pre_g[...] = jnp.dot(n2[...], wg[:, cut], preferred_element_type=F32)
             pre_u[...] = jnp.dot(n2[...], wu[:, cut], preferred_element_type=F32)
-            grad_h[...] = lax.dot_general(cot_here, wd[cut, :], NT, preferred_element_type=F32)
             if t + TILE == 2304:
                 relay("x")
                 relay("y")
 
-            def act_rows(r, carry):
+            def act_rows(r, carry, t=t):
                 here = pl.ds(r, 32)
-                gate, up, grad = pre_g[here, :], pre_u[here, :], grad_h[here, :]
+                gate, up, grad = pre_g[here, :], pre_u[here, :], grad_h[t // TILE, here, :]
                 sig = jax.nn.sigmoid(gate)
                 act = gate * sig
-                hid_s[here, :] = (act * up).astype(BF16)
+                hid_s[here, t:t + TILE] = (act * up).astype(BF16)
                 gg_s[here, :] = (grad * up * (sig * (1.0 + gate * (1.0 - sig)))).astype(BF16)
                 ug_s[here, :] = (grad * act).astype(BF16)
                 return carry
 
             in_rows(256, 32, act_rows)
-            hidt[cut, :] = hid_s[...].T
+            hidt[cut, :] = hid_s[:, cut].T
             gatet[cut, :] = gg_s[...].T
             upt[cut, :] = ug_s[...].T
-            ffn = jnp.dot(hid_s[...], wd[cut, :], preferred_element_type=F32)
+            last = t + TILE == 2304
+            if last:
+                for copy in traded.values():
+                    copy.start()
             back = lax.dot_general(gg_s[...], wg[:, cut], NT, preferred_element_type=F32)
             back += lax.dot_general(ug_s[...], wu[:, cut], NT, preferred_element_type=F32)
-            last = t + TILE == 2304
             if t > 0:
-                ffn += ffn_acc[...]
                 back += n2g_acc[...]
             if last:
                 xn[0] = back.astype(BF16)
-                xf[0] = ffn.astype(BF16)
             else:
-                ffn_acc[...] = ffn
                 n2g_acc[...] = back
+        back_link.start()
+        xf[0] = jnp.dot(hid_s[...], wd[...], preferred_element_type=F32).astype(BF16)
+        ffn_link.start()
         links.close()
 
     v = lambda *shape: pltpu.VMEM(shape, BF16)
     f = lambda *shape: pltpu.VMEM(shape, F32)
     pl.run_scoped(
         forward, v(1024, 2304), v(1024, 2304), v(2304, 1024),
-        f(256, TILE), f(256, TILE), f(256, TILE), v(256, TILE), v(256, TILE), v(256, TILE),
-        f(256, 1024), f(256, 1024),
+        f(256, TILE), f(256, TILE), f(3, 256, TILE), v(256, 2304), v(256, TILE), v(256, TILE),
+        f(256, 1024),
     )
 
     def backward(g1, g2, u1, u2, d1, dt, d2, ia, ib, ic, ja, jb, jc, ka, kb, kc, oa, ob, oc):
-        back_link = links.send(xn.at[0], xn.at[1], place.sibling())
-        trade("z", hidt, hz)
-        trade("x", gatet, gx)
-        trade("y", upt, uy)
-        ffn_link = links.send(xf.at[0], xf.at[1], place.sibling())
         share("z", cotz)
         back_link.wait_recv()
         ffn_link.wait_recv()
@@ -542,6 +550,8 @@
         sm2[1] = sm2[0] + sm1[1, 0] + sm1[1, 1] + sm1[1, 2]
         small_links = [links.send(sm2.at[1], sm1.at[2, shift - 1], place.peer("y", shift)) for shift in (1, 3, 2)]
 
+        for ring in in_rings:
+            ring.pass_on()
         dt[pl.ds(144, 16), :] = jnp.zeros((16, 1024), F32)
         for half in range(2):
             dt[pl.ds(0, 144), half * 512:(half + 1) * 512] = down_ring.total(half).reshape(144, 512)
@@ -554,15 +564,6 @@
         for half in range(2):
             g2[pl.ds(2 * half, 2)] = gate_ring.total(half).astype(BF16).reshape(2, 4, 16, 576)
         gate_plane = Plane(place, links, "zx", g2, g3)
-        for half in range(2):
-            u2[pl.ds(2 * half, 2)] = up_ring.total(half).astype(BF16).reshape(2, 4, 16, 576)
-        up_plane = Plane(place, links, "xy", u2, u3)
-
-        for ring in in_rings:
-            ring.pass_on()
-        for copy in small_links:
-            copy.wait_recv()
-        small_out[...] = sm2[1] + sm1[2, 0] + sm1[2, 1] + sm1[2, 2]
         in_links = []
         lines = (("y", ic, i3), ("z", jc, j3), ("x", kc, k3), ("y", oc, o3))
         for ring, (axis, own, got) in zip(in_rings, lines):
@@ -571,6 +572,13 @@
             for shift in (2, 1, 3):
                 there = own.at[place.blocks[axis][shift]]
                 in_links.append(links.send(there, got.at[shift - 1], place.peer(axis, shift)))
+        for half in range(2):
+            u2[pl.ds(2 * half, 2)] = up_ring.total(half).astype(BF16).reshape(2, 4, 16, 576)
+        up_plane = Plane(place, links, "xy", u2, u3)
+
+        for copy in small_links:
+            copy.wait_recv()
+        small_out[...] = sm2[1] + sm1[2, 0] + sm1[2, 1] + sm1[2, 2]
         for copy in down_links:
             copy.wait_recv()
         res = d2[place.coord["y"]].astype(F32)
@@ -595,7 +603,7 @@
         out_out[:, 0:512] = sums[3][:8]
         out_out[:, 512:1024] = sums[3][8:]
         links.close()
-        for copy in gathered.values():
+        for copy in (*gathered.values(), *traded.values(), back_link, ffn_link):
             copy.wait_send()
 
     pl.run_scoped(

time: 96.8 us -> 95.7 us (0.989)
  Pallas kernels: 95.8 us -> 94.7 us
    pallas_call x1, Pallas kernels: 93.2 us -> 92.1 us  [shards(): pl.pallas_call(block_kernel, out_shape=[jax.ShapeDtypeStruct((256, 1024),...]
where the time goes in v4:
time: 95.7 us; the launch traced here: 95.5 us
  Pallas kernels  94.7 us (99%)
    pallas_call x1, Pallas kernels, shards(): pl.pallas_call(block_kernel, out_shape=[jax.ShapeDtypeStruct((256, 1024),...  92.1 us
    pallas_call x1, Pallas kernels, shards(): pl.pallas_call(finish_kernel, out_shape=[jax.ShapeDtypeStruct((256, 1024)...  2.64 us

profile of v4, /device:TPU:0, one launch (start us, length us, event | category | flops | bytes accessed | tf_op | source)
XLA Modules:
  0.0 95.5 jit_solution(5993690576931316307)
XLA Ops:
  0.6 92.1 %block.1 = (bf16[256,1024]{1,0:T(8,128)(2,1)}, bf16[256,1024]{1,0:T(8,128)(2,1)}, f32[16,2304]{1,0:T(8,128)}, f32[16,2304]{1,0:T(8,128)}, f32[36,1024]{1,0:T(8,1...) custom-call(bf16[256,1024]{1,0:T(8,128)(2,1)} %hin.1, f32[1,1024]{1,0:T(1,128)} %bitcast.12, ...), custom_call_target="tpu_custom_call" | custom-call | tf_op jit(solution)/shard_map/block/pallas_call | solution.py:666
  92.7 2.6 %finish.1 = (bf16[256,1024]{1,0:T(8,128)(2,1)}, bf16[256,1024]{1,0:T(8,128)(2,1)}, f32[16,2304]{1,0:T(8,128)}, f32[16,2304]{1,0:T(8,128)}, f32[36,1024]{1,0:T(8,...) custom-call(bf16[256,1024]{1,0:T(8,128)(2,1)} %get-tuple-element.28., ...), custom_call_target="tpu_custom_call" | custom-call | tf_op jit(solution)/shard_map/finish/pallas_call | solution.py:687

commit v5 on v4

--- a/solution.py
+++ b/solution.py
@@ -388,6 +388,14 @@
 
         total = lax.fori_loop(0, 8, norm_two_back, jnp.zeros((8, 1024), F32))
         small[1:2, :] = jnp.sum(total, axis=0, keepdims=True)
+        def out_tile(i, carry):
+            res = jnp.dot(mixedt[i], mlow[...], preferred_element_type=F32)
+            oa[i] = res.astype(BF16).reshape(8, 16, 1024)
+            return carry
+
+        lax.fori_loop(0, 4, out_tile, 0)
+        out_ring = Ring(place, links, "z", halves_of(oa, 0, 1), oa1, oa2)
+        out_ring.start()
         mxg[...] = lax.dot_general(mlow[...], wout[...], NT, preferred_element_type=F32)
 
         def conv_back(r, totals):
@@ -405,14 +413,6 @@
         for k in range(3):
             small[2 + k:3 + k, 0:512] = jnp.sum(totals[k], axis=0, keepdims=True)
 
-        def out_tile(i, carry):
-            res = jnp.dot(mixedt[i], mlow[...], preferred_element_type=F32)
-            oa[i] = res.astype(BF16).reshape(8, 16, 1024)
-            return carry
-
-        lax.fori_loop(0, 4, out_tile, 0)
-        out_ring = Ring(place, links, "z", halves_of(oa, 0, 1), oa1, oa2)
-        out_ring.start()
         edge.wait_recv()
         cgbuf[pl.ds(256, 8), :] = cgbuf[pl.ds(256, 8), :] * carried_on
 

time: 95.7 us -> 96.4 us (level)
  no operation moved by 1% of the time
where the time goes in v5:
time: 96.4 us; the launch traced here: 96.2 us
  Pallas kernels  95.4 us (99%)
    pallas_call x1, Pallas kernels, shards(): pl.pallas_call(block_kernel, out_shape=[jax.ShapeDtypeStruct((256, 1024),...  92.8 us
    pallas_call x1, Pallas kernels, shards(): pl.pallas_call(finish_kernel, out_shape=[jax.ShapeDtypeStruct((256, 1024)...  2.64 us

profile of v5, /device:TPU:0, one launch (start us, length us, event | category | flops | bytes accessed | tf_op | source)
XLA Modules:
  0.0 96.2 jit_solution(2861966825915303455)
XLA Ops:
  0.6 92.8 %block.1 = (bf16[256,1024]{1,0:T(8,128)(2,1)}, bf16[256,1024]{1,0:T(8,128)(2,1)}, f32[16,2304]{1,0:T(8,128)}, f32[16,2304]{1,0:T(8,128)}, f32[36,1024]{1,0:T(8,1...) custom-call(bf16[256,1024]{1,0:T(8,128)(2,1)} %hin.1, f32[1,1024]{1,0:T(1,128)} %bitcast.12, ...), custom_call_target="tpu_custom_call" | custom-call | tf_op jit(solution)/shard_map/block/pallas_call | solution.py:666
  93.4 2.6 %finish.1 = (bf16[256,1024]{1,0:T(8,128)(2,1)}, bf16[256,1024]{1,0:T(8,128)(2,1)}, f32[16,2304]{1,0:T(8,128)}, f32[16,2304]{1,0:T(8,128)}, f32[36,1024]{1,0:T(8,...) custom-call(bf16[256,1024]{1,0:T(8,128)(2,1)} %get-tuple-element.28., ...), custom_call_target="tpu_custom_call" | custom-call | tf_op jit(solution)/shard_map/finish/pallas_call | solution.py:687
